TPU v7x, 128 devices: a whole 4x4x4 slice. The times are simulated.
128 devices in a mesh: band: 32 (over x, z, core), level: 4 (over y).
Axes of the slice: x: 4, y: 4, z: 4, core: 2. Of those that a mesh axis runs over, the one named last changes fastest.
Arguments:
- lower_nodes: bfloat16 [393216, 64], P(('band', 'level')), may hold values from -6 to 6
- latent: bfloat16 [98304, 64], P(('band', 'level')), may hold values from -6 to 6
- up_feat: bfloat16 [786432, 64], P(('band', 'level')), may hold values from -6 to 6
- down_feat: bfloat16 [786432, 64], P(('band', 'level')), may hold values from -6 to 6
- up_send: int32 [1536, 128], P(('band', 'level')), may hold values from 0 to 3071
- up_counts: int32 [128, 12], P(('band', 'level')), may hold values from 0 to 128, as said below
- up_senders: int32 [786432], P(('band', 'level')), may hold values from 0 to 1535, as said below
- up_targets: int32 [786432], P(('band', 'level')), may hold values from 0 to 767
- down_send: int32 [1536, 128], P(('band', 'level')), may hold values from 0 to 767
- down_counts: int32 [128, 12], P(('band', 'level')), may hold values from 0 to 128, as said below
- down_senders: int32 [786432], P(('band', 'level')), may hold values from 0 to 1535, as said below
- down_targets: int32 [786432], P(('band', 'level')), may hold values from 0 to 3071
- edge_w1: bfloat16 [2, 192, 64], replicated, may hold values from -0.4375 to 0.4375
- edge_w2: bfloat16 [2, 64, 64], replicated, may hold values from -0.75 to 0.75
- node_w1: bfloat16 [2, 128, 64], replicated, may hold values from -0.5 to 0.5
- node_w2: bfloat16 [2, 64, 64], replicated, may hold values from -0.75 to 0.75
- biases: float32 [2, 6, 64], replicated, may hold values from -1.5 to 1.5
- norm_gains: float32 [2, 2, 64], replicated, may hold values from 0.5 to 1.5
- lower_cot: float32 [393216, 64], P(('band', 'level')), may hold values from -6 to 6
- upper_cot: float32 [98304, 64], P(('band', 'level')), may hold values from -6 to 6
Outputs:
- lower_out: float32 [393216, 64], P(('band', 'level'))
- upper_out: float32 [98304, 64], P(('band', 'level'))
- grad_lower: float32 [393216, 64], P(('band', 'level'))
- grad_latent: float32 [98304, 64], P(('band', 'level'))
- grad_up_feat: float32 [786432, 64], P(('band', 'level'))
- grad_down_feat: float32 [786432, 64], P(('band', 'level'))
- grad_edge_w1: float32 [2, 192, 64], replicated
- grad_edge_w2: float32 [2, 64, 64], replicated
- grad_node_w1: float32 [2, 128, 64], replicated
- grad_node_w2: float32 [2, 64, 64], replicated
- grad_biases: float32 [2, 6, 64], replicated
- grad_gains: float32 [2, 2, 64], replicated
Inputs may be any that keep to these rules, and one draw needn't show every extreme that they name: `up_counts`: 0 exactly where band (band of d) + k - 1 lies outside the grid, else 1 to 128; 128 in some entry of every row. `up_senders`: every edge reads a live slot: q mod 128 < up_counts[d, q // 128]; the most and 0 are reached. `down_counts`: 0 exactly where band (band of d) + k - 1 lies outside the grid, else 1 to 128; 128 in some entry of every row. `down_senders`: every edge reads a live slot: q mod 128 < down_counts[d, q // 128]; the most and 0 are reached.
All inputs are finite; a program needn't handle non-finite values.
Results may differ from a plain program's by a relative error of at most 0.02.
Values may be sent and summed in bfloat16 or wider, within the bound.
No kernel may reach another device: no remote copies, remote signals or barrier semaphores. Data moves between devices by JAX's collectives and lax.ppermute only.
A program may use at most 128 MiB of HBM per device.

v0:
```python
import functools

import jax
import jax.numpy as jnp
from jax import lax
from jax.experimental import pallas as pl
from jax.experimental.pallas import tpu as pltpu
from jax.sharding import PartitionSpec as P

EPSILON = 1e-05
F32 = jnp.float32
B16 = jnp.bfloat16
D = 64
SLOT_GROUPS, SLOT_COLS = 6, 256
EDGE_BLOCK = 3072
CHUNK = 1024
VMEM_BYTES = 24 * 1024 * 1024


def groups_of(rows):
    return (4, rows // 4) if rows > 1024 else (rows // 256, 256)


def dot(a, b):
    return jnp.dot(a, b, preferred_element_type=F32)


def dot_rows(a, b):
    return lax.dot_general(a, b, (((1,), (1,)), ((), ())), preferred_element_type=F32)


def halves(x):
    high = x.astype(B16)
    return high, (x - high.astype(F32)).astype(B16)


def one_hot(column, n):
    rows = lax.broadcasted_iota(jnp.int16, (n, column.shape[1]), 0)
    return jnp.where(rows == column.astype(jnp.int16), jnp.ones((), B16), jnp.zeros((), B16))


def place(index, groups, n):
    group = jnp.zeros_like(index)
    for j in range(1, groups):
        group = group + (index >= j * n).astype(jnp.int32)
    return group, index - group * n


def level_and_core():
    return lax.axis_index("level").astype(jnp.int32), lax.axis_index("band").astype(jnp.int32) & 1


def band_offsets(swapped):
    unused, core = level_and_core()
    return (2 - 2 * core, 2 * core, 1) if swapped else (0, 2, 1)


def slot_place(senders, swapped):
    level, unused = level_and_core()
    distance = (level - ((senders >> 7) & 3)) & 3
    offset = senders >> 9
    source = jnp.where(offset == 1, 2, jnp.where(offset == band_offsets(swapped)[0], 0, 1))
    block = distance * 3 + source
    return block >> 1, ((block & 1) << 7) | (senders & 127)


def live(senders, counts_ref):
    peer = senders >> 7
    limit = jnp.zeros_like(senders)
    for j in range(12):
        limit = jnp.where(peer == j, counts_ref[0, j], limit)
    return ((senders & 127) < limit).astype(F32)


def choose(stacked, group, groups):
    picked = stacked[0:D]
    for j in range(1, groups):
        picked = jnp.where(group == j, stacked[j * D : (j + 1) * D], picked)
    return picked


def row_of(ref, k, start, size):
    rows = size // 128
    if not isinstance(start, int):
        start = pl.multiple_of(start // 128, rows)
        return jnp.concatenate([ref[k, pl.ds(start + r, 1), :] for r in range(rows)], axis=1)
    return jnp.concatenate([ref[k, r : r + 1, :] for r in range(start // 128, start // 128 + rows)], axis=1)


def pick(table, group, column, groups, n):
    return choose(dot(table[...], one_hot(column, n)), group, groups).astype(B16)


def spread(values, group, groups):
    wide = jnp.broadcast_to(group.astype(jnp.int16), values.shape)
    nothing = jnp.zeros_like(values)
    return jnp.concatenate([jnp.where(wide == j, values, nothing) for j in range(groups)], axis=0)


def add_at(total, values, group, column, groups, n):
    total[...] += dot_rows(spread(values, group, groups), one_hot(column, n))


def pack_table(table, source, groups, n):
    for j in range(groups):
        table[j * D : (j + 1) * D, :] = source[:, j * n : (j + 1) * n]


def columns_of(biases_ref, gains_ref, k):
    rows = [biases_ref[i, k : k + 1] for i in range(6)] + [gains_ref[k]]
    return jnp.concatenate(rows, axis=0).T


def fold(values):
    total = values[:, 0:128]
    for i in range(128, values.shape[1], 128):
        total = total + values[:, i : i + 128]
    return total


def norm_parts(values):
    centre = values - jnp.sum(values, axis=0, keepdims=True) * (1.0 / D)
    spread_sum = jnp.sum(centre * centre, axis=0, keepdims=True) * (1.0 / D)
    factor = lax.rsqrt(spread_sum + EPSILON)
    return centre * factor, factor


def norm_back(grad, normed, factor, gain):
    scaled = grad * gain
    first = jnp.sum(scaled, axis=0, keepdims=True) * (1.0 / D)
    second = jnp.sum(scaled * normed, axis=0, keepdims=True) * (1.0 / D)
    return factor * (scaled - first - normed * second)


def sigmoid(values):
    return 0.5 * jnp.tanh(0.5 * values) + 0.5


def send_rows(send_ref, offset):
    level, unused = level_and_core()
    return jnp.concatenate(
        [send_ref[pl.ds(offset * 4 + ((level + d) & 3), 1), :] for d in range(4)], axis=1
    )


def send_blocks(outs, table, send_ref, groups, n, swapped):
    for j, offset in enumerate(band_offsets(swapped)):
        group, column = place(send_rows(send_ref, offset), groups, n)
        rows = pick(table, group, column, groups, n)
        for d in range(4):
            outs[j][d] = rows[:, d * 128 : (d + 1) * 128]


def add_back(total, blocks, send_ref, groups, n, swapped):
    for j, offset in enumerate(band_offsets(swapped)):
        group, column = place(send_rows(send_ref, offset), groups, n)
        values = jnp.concatenate([block_at(blocks, d, j) for d in range(4)], axis=1)
        add_at(total, values, group, column, groups, n)


def block_at(received, d, j):
    return received[j][0] if d == 0 else received[2 + d][j]


def slot_table(table, received):
    for t in range(12):
        table[(t >> 1) * D : ((t >> 1) + 1) * D, (t & 1) * 128 : ((t & 1) + 1) * 128] = block_at(received, t // 3, t % 3)


def slot_gradients(outs, sums, weight):
    for j in range(SLOT_GROUPS):
        high, low = halves(sums[j * D : (j + 1) * D, :])
        grads = (dot(weight, high) + dot(weight, low)).astype(B16)
        for t in (2 * j, 2 * j + 1):
            outs[t % 3][t // 3] = grads[:, (t & 1) * 128 : ((t & 1) + 1) * 128]


def over_blocks(total, block, body):
    block = min(block, total)
    if block == total:
        body(pl.ds(0, block))
        return

    def step(i, carry):
        body(pl.ds(pl.multiple_of(i * block, block), block))
        return carry

    lax.fori_loop(0, total // block, step, 0)


def pipelined(stages, spans):
    held = [None] * len(spans)
    for t in range(len(spans) + len(stages) - 1):
        for k in reversed(range(len(stages))):
            i = t - k
            if 0 <= i < len(spans):
                held[i] = stages[k](spans[i], held[i])


def spans_of(parts, chunk):
    spans, start = [], 0
    for which, ref in enumerate(parts):
        size = min(chunk, ref.shape[1])
        for at in range(0, ref.shape[1], size):
            spans.append((which, pl.ds(at, size), pl.ds(start + at, size)))
        start += ref.shape[1]
    return spans


def tables_kernel(upper_rows, lower_rows, counts_up, counts_down, senders_up, targets_up, senders_down, targets_down,
                  index_up, alive_up, index_down, alive_down, limits_up, limits_down, sems):
    copies = [pltpu.make_async_copy(counts_up, limits_up, sems.at[0]), pltpu.make_async_copy(counts_down, limits_down, sems.at[1])]
    for copy in copies:
        copy.start()
    sweeps = ((index_up, senders_up, targets_up, upper_rows, True), (index_down, senders_down, targets_down, lower_rows, False))
    for index_ref, senders_ref, targets_ref, rows, swapped in sweeps:
        index_ref[0], index_ref[1] = place(targets_ref[...], *groups_of(rows))
        index_ref[2], index_ref[3] = slot_place(senders_ref[...], swapped)
    for copy in copies:
        copy.wait()
    alive_up[0] = live(senders_up[...], limits_up)
    alive_down[0] = live(senders_down[...], limits_down)


def send_kernel(count, *refs):
    sources, refs = refs[:count], refs[count:]
    sent, held, table, sems = refs[:3], refs[3:-2], refs[-2], refs[-1]
    copies = [pltpu.make_async_copy(a, b, sems.at[i]) for i, (a, b) in enumerate(zip(sources, held))]
    for copy in copies:
        copy.start()
    for copy in copies[:2]:
        copy.wait()
    send_ref, source_ref = held[:2]
    groups, n = groups_of(source_ref.shape[1])
    pack_table(table, source_ref, groups, n)
    send_blocks(sent, table, send_ref, groups, n, True)
    for copy in copies[2:]:
        copy.wait()


def part_kernel(k, block, index_ref, feat_ref, local_ref, w1_ref, biases_ref, gains_ref, *rest):
    part_ref, rows_ref, table, sem = rest[-4:]
    copy = pltpu.make_async_copy(feat_ref, rows_ref.at[0:D], sem)
    copy.start()
    groups, n = groups_of(local_ref.shape[1])
    pack_table(table, local_ref, groups, n)
    columns = columns_of(biases_ref, gains_ref, k)
    weight = jnp.concatenate([w1_ref[k, :, 0:D], w1_ref[k, :, 2 * D : 3 * D]], axis=1)

    def body(s):
        rows_ref[D : 2 * D, s] = pick(table, row_of(index_ref, 0, s.start, s.size), row_of(index_ref, 1, s.start, s.size), groups, n)

    over_blocks(feat_ref.shape[1], block, body)
    copy.wait()
    part_ref[...] = dot(weight, rows_ref[...]) + columns[:, 0:1]


def edges_forward(k, parts, alive_ref, index_ref, table, w1_ref, w2_ref, columns, total, groups, n,
                  slope_ref, normed_ref, hidden_ref, factor_ref):
    weight_slot = w1_ref[k, :, D : 2 * D]
    weight_two = w2_ref[k].astype(F32).T.astype(B16)
    total[...] = jnp.zeros_like(total)

    def slot_rows(span, unused):
        a, size = span[2].start, span[2].size
        return pick(table, row_of(index_ref, 2, a, size), row_of(index_ref, 3, a, size), SLOT_GROUPS, SLOT_COLS)

    def first_layer(span, picked):
        which, t, s = span
        first = parts[which][:, t] + dot(weight_slot, picked)
        gate = sigmoid(first)
        hidden = (first * gate).astype(B16)
        slope_ref[:, s] = gate * (1.0 + first * (1.0 - gate))
        hidden_ref[:, s] = hidden
        return hidden

    def second_layer(span, hidden):
        s = span[2]
        normed, factor = norm_parts(dot(weight_two, hidden) + columns[:, 1:2])
        alive = row_of(alive_ref, 0, s.start, s.size)
        normed_ref[:, s] = normed
        factor_ref[:, s] = factor
        return ((normed * columns[:, 6:7] + columns[:, 2:3]) * alive).astype(B16)

    def sum_messages(span, messages):
        a, size = span[2].start, span[2].size
        add_at(total, messages, row_of(index_ref, 0, a, size), row_of(index_ref, 1, a, size), groups, n)

    pipelined((slot_rows, first_layer, second_layer, sum_messages), spans_of(parts, CHUNK))


def node_first(k, inputs, wn1_ref, columns):
    first = dot(wn1_ref[k], inputs) + columns[:, 3:4]
    gate = sigmoid(first)
    return (first * gate).astype(B16), gate * (1.0 + first * (1.0 - gate))


def node_second(hidden, weight_two, columns):
    return norm_parts(dot(weight_two, hidden) + columns[:, 4:5])


def node_second_grad(grad, normed, factor, columns, sums_ref):
    sums_ref[2] += fold(grad)
    sums_ref[3] += fold(grad * normed)
    return norm_back(grad, normed, factor, columns[:, 7:8]).astype(B16)


def node_weight_grads(first, second, inputs, hidden, one_ref, two_ref, sums_ref):
    sums_ref[0] += fold(first.astype(F32))
    sums_ref[1] += fold(second.astype(F32))
    one_ref[...] += dot_rows(first, inputs)
    two_ref[...] += dot_rows(hidden, second)


def clear(refs):
    for ref in refs:
        ref[...] = jnp.zeros_like(ref)


def transposed(weight):
    return weight.astype(F32).T.astype(B16)


def edge_second(grad_rows, s, columns, weight_sum, alive_ref, normed_ref, factor_ref, sums_ref):
    grad = dot(weight_sum, grad_rows) * row_of(alive_ref, 0, s.start, s.size)
    normed = normed_ref[:, s]
    sums_ref[2] += fold(grad)
    sums_ref[3] += fold(grad * normed)
    return norm_back(grad, normed, factor_ref[:, s], columns[:, 6:7]).astype(B16)


def edge_first(second, s, weight_two, slope_ref):
    return (dot(weight_two, second) * slope_ref[:, s]).astype(B16)


def edge_weight_grads(first, second, rows, hidden, one_ref, two_ref, sums_ref):
    sums_ref[0] += fold(first.astype(F32))
    sums_ref[1] += fold(second.astype(F32))
    one_ref[...] += dot_rows(first, rows)
    two_ref[...] += dot_rows(hidden, second)


def pack_columns(edge_sums, node_sums):
    order = (edge_sums[0], edge_sums[1], edge_sums[2], node_sums[0], node_sums[1], node_sums[2], edge_sums[3], node_sums[3])
    columns = [jnp.sum(v, axis=1, keepdims=True) for v in order]
    lanes = lax.broadcasted_iota(jnp.int32, (D, D), 1)
    packed = jnp.zeros((D, D), F32)
    for i, column in enumerate(columns):
        packed = jnp.where(lanes == i, column, packed)
    return packed


def slot_weight_grads(sums, table):
    total = jnp.zeros((D, D), F32)
    for j in range(SLOT_GROUPS):
        high, low = halves(sums[j * D : (j + 1) * D, :])
        rows = table[j * D : (j + 1) * D, :]
        total = total + dot_rows(high, rows) + dot_rows(low, rows)
    return total


def target_grads(total, weight, start, out_ref, groups, n):
    for j in range(groups):
        high, low = halves(total[j * D : (j + 1) * D, :])
        out_ref[:, j * n : (j + 1) * n] = start(j) + dot(weight, high) + dot(weight, low)


def up_forward_kernel(part_ref, alive_ref, index_ref, r0, r1, r2, r3, r4, r5, local_ref, send_ref,
                      w1_ref, w2_ref, wn1_ref, wn2_ref, biases_ref, gains_ref,
                      out_ref, summed_ref, s0, s1, s2, slope_ref, normed_ref, hidden_ref, factor_ref,
                      slots, total, table, out, sem):
    groups, n = groups_of(local_ref.shape[1])
    columns = columns_of(biases_ref, gains_ref, 0)
    slot_table(slots, (r0, r1, r2, r3, r4, r5))
    edges_forward(0, (part_ref,), alive_ref, index_ref, slots, w1_ref, w2_ref, columns, total, groups, n,
                  slope_ref, normed_ref, hidden_ref, factor_ref)
    weight_two = transposed(wn2_ref[0])

    def first_layer(j, unused):
        s = slice(j * n, (j + 1) * n)
        summed = total[j * D : (j + 1) * D, :].astype(B16)
        summed_ref[:, s] = summed
        return node_first(0, jnp.concatenate([local_ref[:, s], summed], axis=0), wn1_ref, columns)

    def second_layer(j, held):
        s = slice(j * n, (j + 1) * n)
        normed, unused = node_second(held[0], weight_two, columns)
        result = local_ref[:, s].astype(F32) + normed * columns[:, 7:8] + columns[:, 5:6]
        out[:, s] = result
        table[j * D : (j + 1) * D, :] = result.astype(B16)

    pipelined((first_layer, second_layer), range(groups))
    copy = pltpu.make_async_copy(out, out_ref, sem)
    copy.start()
    send_blocks((s0, s1, s2), table, send_ref, groups, n, False)
    copy.wait()


def down_kernel(part_ref, alive_ref, index_ref, r0, r1, r2, r3, r4, r5, local_ref, cot_ref,
                w1_ref, w2_ref, wn1_ref, wn2_ref, biases_ref, gains_ref,
                out_ref, g0, g1, g2, first_ref, second_ref, hidden_ref, sums_ref, edge_sums, node_sums,
                table, summed_ref, node_hidden_ref, node_second_ref,
                slots, total, slope_ref, normed_ref, factor_ref, out, sem):
    groups, n = groups_of(local_ref.shape[1])
    columns = columns_of(biases_ref, gains_ref, 1)
    slot_table(slots, (r0, r1, r2, r3, r4, r5))
    parts = (part_ref,)
    edges_forward(1, parts, alive_ref, index_ref, slots, w1_ref, w2_ref, columns, total, groups, n,
                  slope_ref, normed_ref, hidden_ref, factor_ref)
    clear((node_sums, edge_sums, sums_ref))
    wn2 = wn2_ref[1]
    wn2_t = transposed(wn2)
    wn1 = transposed(wn1_ref[1])

    def first_layer(j, unused):
        summed = total[j * D : (j + 1) * D, :].astype(B16)
        summed_ref[j * D : (j + 1) * D, :] = summed
        inputs = jnp.concatenate([local_ref[:, j * n : (j + 1) * n], summed], axis=0)
        return node_first(1, inputs, wn1_ref, columns)

    def second_layer(j, held):
        hidden, slope = held
        s = slice(j * n, (j + 1) * n)
        normed, factor = node_second(hidden, wn2_t, columns)
        out[:, s] = local_ref[:, s].astype(F32) + normed * columns[:, 7:8] + columns[:, 5:6]
        second = node_second_grad(cot_ref[:, s], normed, factor, columns, node_sums)
        node_hidden_ref[:, s] = hidden
        node_second_ref[:, s] = second
        return slope, second

    def node_grads(j, held):
        slope, second = held
        table[j * D : (j + 1) * D, :] = (dot(wn2, second) * slope).astype(B16)

    pipelined((first_layer, second_layer, node_grads), range(groups))
    copy = pltpu.make_async_copy(out, out_ref, sem)
    copy.start()
    weight_two = w2_ref[1]
    weight_slot = transposed(w1_ref[1, :, D : 2 * D])

    def grad_rows(span, unused):
        a, size = span[2].start, span[2].size
        return pick(table, row_of(index_ref, 0, a, size), row_of(index_ref, 1, a, size), groups, n)

    def second_grad(span, rows):
        return edge_second(rows, span[2], columns, wn1[D : 2 * D], alive_ref, normed_ref, factor_ref, edge_sums)

    def first_grad(span, second):
        s = span[2]
        first = edge_first(second, s, weight_two, slope_ref)
        first_ref[:, s] = first
        second_ref[:, s] = second
        return first

    def sum_slots(span, first):
        a, size = span[2].start, span[2].size
        add_at(sums_ref, first, row_of(index_ref, 2, a, size), row_of(index_ref, 3, a, size), SLOT_GROUPS, SLOT_COLS)

    pipelined((grad_rows, second_grad, first_grad, sum_slots), spans_of(parts, CHUNK))
    slot_gradients((g0, g1, g2), sums_ref, weight_slot)
    copy.wait()


def down_targets_kernel(index_ref, first_ref, cot_ref, table, w1_ref, wn1_ref, *rest):
    grad_ref, total = rest[-2:]
    groups, n = groups_of(cot_ref.shape[1])
    weight = transposed(w1_ref[1, :, 2 * D : 3 * D])
    total[...] = jnp.zeros_like(total)

    def body(s):
        group, column = row_of(index_ref, 0, s.start, s.size), row_of(index_ref, 1, s.start, s.size)
        add_at(total, first_ref[:, s], group, column, groups, n)

    over_blocks(first_ref.shape[1], EDGE_BLOCK, body)
    weight_node = transposed(wn1_ref[1, :, 0:D])

    def start(j):
        return cot_ref[:, j * n : (j + 1) * n] + dot(weight_node, table[j * D : (j + 1) * D, :])

    target_grads(total, weight, start, grad_ref, groups, n)


def down_rest_kernel(rows_ref, first_ref, second_ref, hidden_ref, r0, r1, r2, r3, r4, r5, sums_ref, edge_in, node_in,
                     table, summed_ref, node_hidden_ref, node_second_ref, local_ref, w1_ref, *rest):
    feat_grad_ref, packed_ref, slots, one_ref, two_ref, wn1_grad, wn2_grad, edge_sums, node_sums = rest[-9:]
    step = pl.program_id(0)
    weight = transposed(w1_ref[1, :, 0:D])

    @pl.when(step == 0)
    def _():
        clear((one_ref, two_ref, wn1_grad, wn2_grad))
        edge_sums[...] = edge_in[...]
        node_sums[...] = node_in[...]

    s = pl.ds(pl.multiple_of(step * EDGE_BLOCK, EDGE_BLOCK), EDGE_BLOCK)
    first = first_ref[:, s]
    feat_grad_ref[...] = dot(weight, first)
    edge_weight_grads(first, second_ref[:, s], rows_ref[:, s], hidden_ref[:, s], one_ref, two_ref, edge_sums)

    @pl.when(step == pl.num_programs(0) - 1)
    def _():
        groups, n = groups_of(local_ref.shape[1])
        for j in range(groups):
            t, rows = slice(j * n, (j + 1) * n), slice(j * D, (j + 1) * D)
            inputs = jnp.concatenate([local_ref[:, t], summed_ref[rows, :]], axis=0)
            node_weight_grads(table[rows, :], node_second_ref[:, t], inputs, node_hidden_ref[:, t], wn1_grad, wn2_grad, node_sums)
        slot_table(slots, (r0, r1, r2, r3, r4, r5))
        write_packed(packed_ref, one_ref[...], slot_weight_grads(sums_ref, slots), two_ref[...],
                     wn1_grad[...], wn2_grad[...], pack_columns(edge_sums, node_sums))


def write_packed(packed_ref, one, slot_grads, two, wn1_grad, wn2_grad, columns):
    packed_ref[0] = jnp.concatenate([one[:, 0:D], slot_grads], axis=1)
    packed_ref[1] = jnp.concatenate([one[:, D : 2 * D], two], axis=1)
    packed_ref[2] = wn1_grad
    packed_ref[3] = jnp.concatenate([wn2_grad, columns], axis=1)


def up_backward_kernel(index_ref, rows_ref, h0, h1, h2, h3, h4, h5,
                       send_ref, cot_ref, local_ref, summed_ref, r0, r1, r2, r3, r4, r5, slope_ref, normed_ref, hidden_ref, factor_ref, alive_ref, packed_down_ref,
                       w1_ref, w2_ref, wn1_ref, wn2_ref, biases_ref, gains_ref,
                       partner_ref, cross_ref, own_ref, first_ref, grad_ref, keep_ref,
                       slots, table, back, total, sums, start, one_ref, two_ref, edge_sums, node_sums, wn1_grad, wn2_grad, pieces):
    groups, n = groups_of(local_ref.shape[1])
    columns = columns_of(biases_ref, gains_ref, 0)
    clear((back, total, sums, one_ref, two_ref, edge_sums, node_sums, wn1_grad, wn2_grad))
    slot_table(slots, (r0, r1, r2, r3, r4, r5))
    add_back(back, (h0, h1, h2, h3, h4, h5), send_ref, groups, n, False)
    wn2 = wn2_ref[0]
    wn2_t = transposed(wn2)
    wn1 = transposed(wn1_ref[0])
    w1 = transposed(w1_ref[0])

    def first_layer(j, unused):
        s = slice(j * n, (j + 1) * n)
        inputs = jnp.concatenate([local_ref[:, s], summed_ref[:, s]], axis=0)
        return inputs, *node_first(0, inputs, wn1_ref, columns)

    def second_layer(j, held):
        inputs, hidden, slope = held
        grad = cot_ref[:, j * n : (j + 1) * n] + back[j * D : (j + 1) * D, :]
        normed, factor = node_second(hidden, wn2_t, columns)
        return inputs, hidden, slope, grad, node_second_grad(grad, normed, factor, columns, node_sums)

    def node_grads(j, held):
        inputs, hidden, slope, grad, second = held
        first = (dot(wn2, second) * slope).astype(B16)
        node_weight_grads(first, second, inputs, hidden, wn1_grad, wn2_grad, node_sums)
        table[j * D : (j + 1) * D, :] = first
        start[:, j * n : (j + 1) * n] = grad + dot(wn1[0:D], first)

    pipelined((first_layer, second_layer, node_grads), range(groups))
    weight_two = w2_ref[0]

    def grad_rows(span, unused):
        a, size = span[2].start, span[2].size
        return pick(table, row_of(index_ref, 0, a, size), row_of(index_ref, 1, a, size), groups, n)

    def second_grad(span, rows):
        return edge_second(rows, span[2], columns, wn1[D : 2 * D], alive_ref, normed_ref, factor_ref, edge_sums)

    def first_grad(span, second):
        s = span[2]
        first = edge_first(second, s, weight_two, slope_ref)
        first_ref[:, s] = first
        edge_weight_grads(first, second, rows_ref[:, s], hidden_ref[:, s], one_ref, two_ref, edge_sums)
        return first

    def sum_rows(span, first):
        s = span[2]
        rows = [row_of(index_ref, i, s.start, s.size) for i in range(4)]
        add_at(total, first, rows[0], rows[1], groups, n)
        add_at(sums, first, rows[2], rows[3], SLOT_GROUPS, SLOT_COLS)

    pipelined((grad_rows, second_grad, first_grad, sum_rows), spans_of((first_ref,), CHUNK))
    slot_gradients((partner_ref, cross_ref, own_ref), sums, w1[D : 2 * D])
    target_grads(total, w1[2 * D : 3 * D], lambda j: start[:, j * n : (j + 1) * n], grad_ref, groups, n)
    slot_grads = slot_weight_grads(sums, slots)
    write_packed(pieces, one_ref[...], slot_grads, two_ref[...], wn1_grad[...], wn2_grad[...],
                 pack_columns(edge_sums, node_sums))
    unused, core = level_and_core()
    for p in range(4):
        pieces[4 + p] = packed_down_ref[p]
    for p in range(4):
        keep_ref[p] = pieces[core * 4 + p]
        partner_ref[4 + p] = pieces[(1 - core) * 4 + p].astype(B16)


def feat_grad_kernel(first_ref, w1_ref, *rest):
    out_ref = rest[-1]
    out_ref[...] = dot(transposed(w1_ref[0, :, 0:D]), first_ref[...])


def lower_grad_kernel(h0, h1, h2, h3, h4, h5, send_ref, start_ref, out_ref, total):
    groups, n = groups_of(start_ref.shape[1])
    clear((total,))
    add_back(total, (h0, h1, h2, h3, h4, h5), send_ref, groups, n, True)
    for j in range(groups):
        s = slice(j * n, (j + 1) * n)
        out_ref[:, s] = start_ref[:, s] + total[j * D : (j + 1) * D, :]


def unpack_kernel(own_ref, other_ref, w1_ref, w2_ref, wn1_ref, wn2_ref, biases_ref, gains_ref, pieces):
    unused, core = level_and_core()
    for p in range(4):
        pieces[core * 4 + p] = own_ref[p].astype(F32)
        pieces[(1 - core) * 4 + p] = other_ref[p].astype(F32)
    for k in range(2):
        w1_ref[k] = jnp.concatenate([pieces[4 * k], pieces[4 * k + 1, :, 0:D]], axis=1)
        w2_ref[k] = pieces[4 * k + 1, :, D : 2 * D]
        wn1_ref[k] = pieces[4 * k + 2]
        wn2_ref[k] = pieces[4 * k + 3, :, 0:D]
        rows = pieces[4 * k + 3].T
        for i in range(6):
            biases_ref[i, k : k + 1] = rows[D + i : D + i + 1]
        gains_ref[k] = rows[D + 6 : D + 8]


def shape(dims, dtype=F32):
    return jax.ShapeDtypeStruct(dims, dtype)


def call(kernel, name, outs, scratch, scalars=0, stored=(), streamed=None, final=(), raw=()):
    steps, stream_in, stream_out = streamed if streamed else (1, (), ())

    def run(*operands, after=()):
        def whole(space):
            return pl.BlockSpec(memory_space=space)

        def cut(x):
            return pl.BlockSpec((x.shape[0], x.shape[1] // steps), lambda i: (0, i))

        in_specs, placed = [], []
        for i, x in enumerate(operands):
            if i < scalars:
                in_specs.append(whole(pltpu.SMEM))
            elif i in stream_in:
                in_specs.append(cut(x))
            elif i in raw:
                in_specs.append(whole(pltpu.HBM))
                x = pltpu.with_memory_space_constraint(x, pltpu.HBM)
            else:
                in_specs.append(whole(pltpu.VMEM))
                x = pltpu.with_memory_space_constraint(x, pltpu.VMEM)
            placed.append(x)
        in_specs += [whole(pl.ANY) for _ in after]
        out_specs, out_shape = [], []
        for i, x in enumerate(outs):
            if i in stream_out:
                out_specs.append(cut(x))
                out_shape.append(x)
            elif i in stored:
                out_specs.append(whole(pl.ANY))
                out_shape.append(x)
            elif i in final:
                out_specs.append(whole(pltpu.VMEM))
                out_shape.append(x)
            else:
                out_specs.append(whole(pltpu.VMEM))
                out_shape.append(pltpu.VMEM(x.shape, x.dtype))
        return pl.pallas_call(
            kernel,
            name=name,
            grid=(steps,) if streamed else (),
            in_specs=in_specs,
            out_specs=out_specs,
            out_shape=out_shape,
            scratch_shapes=scratch,
            compiler_params=pltpu.CompilerParams(vmem_limit_bytes=VMEM_BYTES),
        )(*placed, *after)

    return run


def core_swap(block):
    return lax.ppermute(block, "band", [(i, i ^ 1) for i in range(lax.axis_size("band"))])


def cross_swap(block):
    last = lax.axis_size("band") - 1
    pairs = [(i, i + 1) for i in range(1, last, 2)]
    return lax.ppermute(block, "band", pairs + [(b, a) for a, b in pairs] + [(0, 0), (last, last)])


def along_level(block, step):
    count = lax.axis_size("level")
    return lax.ppermute(block, "level", [(i, (i + step) % count) for i in range(count)])


def along_band(block, step):
    count = lax.axis_size("band")
    return lax.ppermute(block, "band", [(i, (i + step) % count) for i in range(count)])


def across_bands(blocks):
    below, above, own = blocks
    return [along_band(above, 1), along_band(below, -1), own]


def along_levels(blocks, sign):
    return blocks + [along_level(jnp.stack([b[d] for b in blocks]), sign * d) for d in (1, 2, 3)]


def chip_ring(block, step, core_strides):
    count = lax.axis_size("band")
    pairs = []
    for i in range(count):
        stride = core_strides[i % 2]
        at = (i // stride) % 4
        pairs.append((i, i + (((at + step) % 4) - at) * stride))
    return lax.ppermute(block, "band", pairs)


def rounded(values):
    return lax.reduce_precision(values, 8, 7)


def sum_of_four(values, first, second, third):
    return (values + second.astype(F32)) + (first.astype(F32) + third.astype(F32))


def sum_along(values, core_strides):
    own = rounded(values)
    sent = own.astype(B16)
    return sum_of_four(own, *(chip_ring(sent, d, core_strides) for d in (1, 2, 3)))


def shards(
    lower_nodes, latent, up_feat, down_feat, up_send, up_counts, up_senders, up_targets,
    down_send, down_counts, down_senders, down_targets,
    edge_w1, edge_w2, node_w1, node_w2, biases, norm_gains, lower_cot, upper_cot,
):
    lower, upper = lower_nodes.T, latent.T
    feat_up, feat_down = up_feat.T, down_feat.T
    cot_lower, cot_upper = lower_cot.T, upper_cot.T
    w1, wn1 = edge_w1.transpose(0, 2, 1), node_w1.transpose(0, 2, 1)
    w2, wn2 = edge_w2, node_w2
    edges, lower_rows, upper_rows = up_feat.shape[0], lower_nodes.shape[0], latent.shape[0]
    dense = (edges // 128, 128)
    senders_up, targets_up, senders_down, targets_down = (
        x.reshape(dense) for x in (up_senders, up_targets, down_senders, down_targets))
    bias_rows = biases.transpose(1, 0, 2)

    lower_groups, lower_n = groups_of(lower_rows)
    upper_groups, upper_n = groups_of(upper_rows)
    lower_table, upper_table = (lower_groups * D, lower_n), (upper_groups * D, upper_n)
    slots = pltpu.VMEM((SLOT_GROUPS * D, SLOT_COLS), B16)
    block, four = shape((4, D, 128), B16), shape((4, D, 128))
    wide32, wide16, row = shape((D, edges)), shape((D, edges), B16), shape((1, edges))
    steps = edges // EDGE_BLOCK

    early = (up_send, lower, senders_up, targets_up, senders_down, targets_down, upper, w1, bias_rows, norm_gains,
             down_send, w2, wn1, wn2)
    count = len(early)
    (*sent, up_send, lower, senders_up, targets_up, senders_down, targets_down, upper, w1, bias_rows,
     norm_gains, down_send, w2, wn1, wn2) = call(
        functools.partial(send_kernel, count), "send_lower", [block] * 3 + [shape(x.shape, x.dtype) for x in early],
        [pltpu.VMEM(lower_table, B16), pltpu.SemaphoreType.DMA((count,))], 0, raw=range(count),
    )(*early)
    index, lives = shape((4, *dense), jnp.int32), shape((1, *dense))
    index_up, alive_up, index_down, alive_down = call(
        functools.partial(tables_kernel, upper_rows, lower_rows), "edge_tables", [index, lives, index, lives],
        [pltpu.SMEM((1, 12), jnp.int32), pltpu.SMEM((1, 12), jnp.int32), pltpu.SemaphoreType.DMA((2,))], 0, raw=(0, 1),
    )(up_counts, down_counts, senders_up, targets_up, senders_down, targets_down)

    def part(k, block, name, table, index, feat, local, after):
        return call(
            functools.partial(part_kernel, k, block), name, [wide32, shape((2 * D, edges), B16)],
            [pltpu.VMEM(table, B16), pltpu.SemaphoreType.DMA], 0, raw=(1,),
        )(index, feat, local, w1, bias_rows, norm_gains, after=after)

    sent = [core_swap(sent[0]), cross_swap(sent[1]), sent[2]]
    sent, alive_up = lax.optimization_barrier((sent, alive_up))
    part_up, rows_up = part(0, EDGE_BLOCK, "part_up", upper_table, index_up, feat_up, upper, (sent[0], sent[1]))
    up_slots = along_levels(sent, 1)
    up_slots, part_up = lax.optimization_barrier((up_slots, part_up))
    (upper_new, summed_up, s0, s1, s2, slope, normed, hidden, factor) = call(
        up_forward_kernel, "up_forward",
        [shape((D, upper_rows)), shape((D, upper_rows), B16)] + [block] * 3 + [wide32, wide32, wide16, row],
        [slots, pltpu.VMEM(upper_table, F32), pltpu.VMEM(upper_table, B16), pltpu.VMEM((D, upper_rows), F32),
         pltpu.SemaphoreType.DMA], 0, (0,),
    )(part_up, alive_up, index_up, *up_slots, upper, down_send, w1, w2, wn1, wn2, bias_rows, norm_gains)
    sent = across_bands([s0, s1, s2])
    part_down, rows_down = part(1, EDGE_BLOCK, "part_down", lower_table, index_down, feat_down, lower, (sent[0], sent[1]))
    down_slots = along_levels(sent, 1)
    down_slots, part_down = lax.optimization_barrier((down_slots, part_down))
    sums_shape = shape((SLOT_GROUPS * D, SLOT_COLS))
    node16 = shape((D, lower_rows), B16)
    (lower_new, g0, g1, g2, first_down, second_down, hidden_down, sums_down, edge_sums, node_sums, *nodes) = call(
        down_kernel, "down_sweep",
        [shape((D, lower_rows))] + [block] * 3 + [wide16] * 3 + [sums_shape, four, four, shape(lower_table, B16),
         shape(lower_table, B16), node16, node16],
        [slots, pltpu.VMEM(lower_table, F32), pltpu.VMEM((D, edges), F32),
         pltpu.VMEM((D, edges), F32), pltpu.VMEM((1, edges), F32),
         pltpu.VMEM((D, lower_rows), F32), pltpu.SemaphoreType.DMA], 0, (0,),
    )(part_down, alive_down, index_down, *down_slots, lower, cot_lower, w1, w2, wn1, wn2, bias_rows, norm_gains)
    back = across_bands([g0, g1, g2])
    feat_grad_down, packed_down = call(
        down_rest_kernel, "down_rest", [wide32, four],
        [slots, pltpu.VMEM((D, 2 * D), F32), pltpu.VMEM((D, D), F32), pltpu.VMEM((D, 2 * D), F32), pltpu.VMEM((D, D), F32),
         pltpu.VMEM((4, D, 128), F32), pltpu.VMEM((4, D, 128), F32)], 0, (), (steps, (), (0,)),
    )(rows_down, first_down, second_down, hidden_down, *down_slots, sums_down, edge_sums, node_sums, *nodes, lower, w1,
      after=(back[0], back[1]))
    down_back = along_levels(back, -1)
    down_back, packed_down = lax.optimization_barrier((down_back, packed_down))
    (partner, cross, own, first_up, grad_latent, keep) = call(
        up_backward_kernel, "up_backward",
        [shape((8, D, 128), B16), block, block, wide16, shape((D, upper_rows)), four],
        [slots, pltpu.VMEM(upper_table, B16), pltpu.VMEM(upper_table, F32), pltpu.VMEM(upper_table, F32),
         pltpu.VMEM((SLOT_GROUPS * D, SLOT_COLS), F32), pltpu.VMEM((D, upper_rows), F32),
         pltpu.VMEM((D, 2 * D), F32), pltpu.VMEM((D, D), F32), pltpu.VMEM((4, D, 128), F32), pltpu.VMEM((4, D, 128), F32),
         pltpu.VMEM((D, 2 * D), F32), pltpu.VMEM((D, D), F32), pltpu.VMEM((8, D, 128), F32)], 0, (), None, (4,),
    )(index_up, rows_up, *down_back, down_send, cot_upper, upper, summed_up, *up_slots,
      slope, normed, hidden, factor, alive_up, packed_down, w1, w2, wn1, wn2, bias_rows, norm_gains)

    partner = core_swap(partner)
    total = rounded(rounded(keep) + partner[4:].astype(F32))
    cross, keep = lax.optimization_barrier((cross, total))
    cross = cross_swap(cross)
    total = sum_along(total, (2, 8))
    (feat_grad_up,) = call(feat_grad_kernel, "feat_grad_up", [wide32], [], 0, (), (steps, (0,), (0,)))(
        first_up, w1, after=(partner,))
    total, cross, feat_grad_up = lax.optimization_barrier((total, cross, feat_grad_up))
    blocks = (partner, cross, own)
    total = rounded(total)
    levels = [
        along_level(jnp.concatenate([jnp.stack([b[d] for b in blocks]), total.astype(B16)]), -d) for d in (1, 2, 3)
    ]
    (start_lower,) = call(
        down_targets_kernel, "down_targets", [shape((D, lower_rows))], [pltpu.VMEM(lower_table, F32)],
    )(index_down, first_down, cot_lower, nodes[0], w1, wn1, after=(total,))
    levels, start_lower = lax.optimization_barrier((levels, start_lower))
    total = sum_of_four(total, *(b[3:] for b in levels))
    (grad_lower,) = call(lower_grad_kernel, "lower_grad", [shape((D, lower_rows))], [pltpu.VMEM(lower_table, F32)], 0, (), None, (0,))(
        *blocks, *levels, up_send, start_lower)
    total = sum_along(total, (8, 2))
    total, grad_lower = lax.optimization_barrier((total, grad_lower))
    total = rounded(total).astype(B16)
    w1_grad, w2_grad, wn1_grad, wn2_grad, bias_grad, gain_grad = call(
        unpack_kernel, "unpack",
        [shape((2, D, 3 * D)), shape((2, D, D)), shape((2, D, 2 * D)), shape((2, D, D)), shape((6, 2, D)), shape((2, 2, D))],
        [pltpu.VMEM((8, D, 128), F32)], 0, (), None, range(6))(total, core_swap(total))
    return (
        lower_new.T, upper_new.T, grad_lower.T, grad_latent.T, feat_grad_up.T, feat_grad_down.T,
        w1_grad.transpose(0, 2, 1), w2_grad, wn1_grad.transpose(0, 2, 1), wn2_grad, bias_grad.transpose(1, 0, 2), gain_grad,
    )


def solution(mesh):
    rows, index, whole = P(("band", "level"), None), P(("band", "level")), P()
    placed = (rows,) * 6 + (index, index) + (rows,) * 2 + (index, index) + (whole,) * 6 + (rows,) * 2
    return jax.shard_map(
        shards,
        mesh=mesh,
        in_specs=placed,
        out_specs=(rows,) * 6 + (whole,) * 6,
        check_vma=False,
    )
```

profile of v0, /device:TPU:1, one launch (start us, length us, event | category | flops | bytes accessed | tf_op | source)
XLA Modules:
  0.0 107.1 jit_solution(9928962017047033915)
XLA Ops:
  0.7 2.0 %send_lower.1 = (bf16[4,64,128]{2,1,0:T(8,128)(2,1)S(1)}, bf16[4,64,128]{2,1,0:T(8,128)(2,1)S(1)}, bf16[4,64,128]{2,1,0:T(8,128)(2,1)S(1)}, s32[12,128]{1,0:T(8,...) custom-call(s32[12,128]{1,0:T(8,128)} %refs_0_.1, ...), custom_call_target="tpu_custom_call" | custom-call | tf_op jit(solution)/shard_map/send_lower/pallas_call | solution.py:661
  4.1 3.5 %collective-permute-start.1 = (bf16[4,64,128]{2,1,0:T(8,128)(2,1)S(1)}, bf16[4,64,128]{2,1,0:T(8,128)(2,1)S(1)}, u32[]{:S(2)}, u32[]{:S(2)}) collective-permute-start(bf16[4,64,128]{2,1,0:T(8,128)(2,1)S(1)} %get-tuple-element.110), channel_id=1, source_target_pairs={{4,8},{12,16},{20,24},{28,32},{36,40},{44,48},{52,56},{60,64},{68,... | collective-permute-start | bytes 196616 | tf_op jit(solution)/shard_map/ppermute | solution.py:682
  9.7 2.9 %collective-permute-start.4 = (bf16[3,64,128]{2,1,0:T(8,128)(2,1)S(1)}, bf16[3,64,128]{2,1,0:T(8,128)(2,1)S(1)}, u32[]{:S(2)}, u32[]{:S(2)}) collective-permute-start(bf16[3,64,128]{2,1,0:T(8,128)(2,1)S(1)} %pad_maximum_fusion.5), channel_id=1, source_target_pairs={{0,3},{1,0},{2,1},{3,2},{4,7},{5,4},{6,5},{7,6},{8,11},{9,8},{10,9... | collective-permute-start | bytes 147464 | tf_op jit(solution)/shard_map/ppermute | solution.py:687
  15.4 1.8 %collective-permute-done.3.r4 = bf16[3,64,128]{2,1,0:T(8,128)(2,1)S(1)} collective-permute-done((bf16[3,64,128]{2,1,0:T(8,128)(2,1)S(1)}, bf16[3,64,128]{2,1,0:T(8,128)(2,1)S(1)}, u32[]{:S(2)}, u32[]{:S(2)}) %collective-permute-start.3) | collective-permute-done | bytes 49184 | tf_op jit(solution)/shard_map/ppermute | solution.py:687
  17.7 5.2 %up_forward.1 = (f32[64,768]{1,0:T(8,128)}, bf16[64,768]{1,0:T(8,128)(2,1)S(1)}, bf16[4,64,128]{2,1,0:T(8,128)(2,1)S(1)}, bf16[4,64,128]{2,1,0:T(8,128)(2,1)S(1)...) custom-call(f32[64,6144]{1,0:T(8,128)S(1)} %get-tuple-element.126.pa, ...), custom_call_target="tpu_custom_call" | custom-call | tf_op jit(solution)/shard_map/up_forward/pallas_call | solution.py:661
  22.9 3.3 %collective-permute-start.5 = (bf16[4,64,128]{2,1,0:T(8,128)(2,1)S(1)}, bf16[4,64,128]{2,1,0:T(8,128)(2,1)S(1)}, u32[]{:S(2)}, u32[]{:S(2)}) collective-permute-start(bf16[4,64,128]{2,1,0:T(8,128)(2,1)S(1)} %get-tuple-element.138), channel_id=1, source_target_pairs={{0,4},{4,8},{8,12},{12,16},{16,20},{20,24},{24,28},{28,32},{32,36}... | collective-permute-start | bytes 196616 | tf_op jit(solution)/shard_map/ppermute | solution.py:692
  27.6 2.4 %collective-permute-done.6.rest_1_.r1 = bf16[4,64,128]{2,1,0:T(8,128)(2,1)S(1)} collective-permute-done((bf16[4,64,128]{2,1,0:T(8,128)(2,1)S(1)}, bf16[4,64,128]{2,1,0:T(8,128)(2,1)S(1)}, u32[]{:S(2)}, u32[]{:S(2)}) %collective-permute-start.6) | collective-permute-done | bytes 65568 | tf_op jit(solution)/shard_map/ppermute | solution.py:692
  32.2 3.3 %part_down.1 = (f32[64,6144]{1,0:T(8,128)S(1)}, bf16[128,6144]{1,0:T(8,128)(2,1)S(1)}) custom-call(s32[4,48,128]{2,1,0:T(8,128)S(1)} %get-tuple-element.141.index_ref, bf16[64,6144]{1,0:T(8,128)(2,1)} %bitcast.27, bf16[64,3072]{1,0:T(8,128)(2,1)S(1)} %get-tuple-element.142.local_ref, bf16[2,64,192]{2,1,0:T(8,128)(2,1)S(1)} %get-tuple-element.122.w1_ref, ...), custom_call_target="tpu_custom_call" | custom-call | tf_op jit(solution)/shard_map/part_down/pallas_call | solution.py:661
  35.7 12.3 %down_sweep.1 = (f32[64,3072]{1,0:T(8,128)}, bf16[4,64,128]{2,1,0:T(8,128)(2,1)S(1)}, bf16[4,64,128]{2,1,0:T(8,128)(2,1)S(1)}, bf16[4,64,128]{2,1,0:T(8,128)(2,1...) custom-call(f32[64,6144]{1,0:T(8,128)S(1)} %get-tuple-element.144.pa, ...), custom_call_target="tpu_custom_call" | custom-call | tf_op jit(solution)/shard_map/down_sweep/pallas_call | solution.py:661
  48.0 2.3 %collective-permute-start.10 = (bf16[4,64,128]{2,1,0:T(8,128)(2,1)S(1)}, bf16[4,64,128]{2,1,0:T(8,128)(2,1)S(1)}, u32[]{:S(2)}, u32[]{:S(2)}) collective-permute-start(bf16[4,64,128]{2,1,0:T(8,128)(2,1)S(1)} %get-tuple-element.155), channel_id=1, source_target_pairs={{0,4},{4,8},{8,12},{12,16},{16,20},{20,24},{24,28},{28,32},{32,36}... | collective-permute-start | bytes 196616 | tf_op jit(solution)/shard_map/ppermute | solution.py:692
  51.7 2.4 %collective-permute-done.11.rest_1_.h1 = bf16[4,64,128]{2,1,0:T(8,128)(2,1)S(1)} collective-permute-done((bf16[4,64,128]{2,1,0:T(8,128)(2,1)S(1)}, bf16[4,64,128]{2,1,0:T(8,128)(2,1)S(1)}, u32[]{:S(2)}, u32[]{:S(2)}) %collective-permute-start.11) | collective-permute-done | bytes 65568 | tf_op jit(solution)/shard_map/ppermute | solution.py:692
  54.2 2.8 %collective-permute-start.13 = (bf16[3,64,128]{2,1,0:T(8,128)(2,1)S(1)}, bf16[3,64,128]{2,1,0:T(8,128)(2,1)S(1)}, u32[]{:S(2)}, u32[]{:S(2)}) collective-permute-start(bf16[3,64,128]{2,1,0:T(8,128)(2,1)S(1)} %pad_maximum_fusion.10), channel_id=1, source_target_pairs={{0,2},{1,3},{2,0},{3,1},{4,6},{5,7},{6,4},{7,5},{8,10},{9,11},{10,... | collective-permute-start | bytes 147464 | tf_op jit(solution)/shard_map/ppermute | solution.py:687
  58.6 3.1 %down_rest.1 = (f32[64,6144]{1,0:T(8,128)}, f32[4,64,128]{2,1,0:T(8,128)S(1)}) custom-call(bf16[128,6144]{1,0:T(8,128)(2,1)S(1)} %get-tuple-element.158.rows_ref, bf16[64,6144]{1,0:T(8,128)(2,1)S(1)} %get-tuple-element.159.first_ref, bf16[64,6144]{1,0:T(8,128)(2,1)S(1)} %get-tuple-element.160.second_ref, bf16[64,6144]{1,0:T(8,128)(2,1)S(1)} %get-tuple-element.161.hidden_ref, ...), custom_call_target="tpu_custom_call" | custom-call | tf_op jit(solution)/shard_map/down_rest/pallas_call | solution.py:661
  61.7 7.3 %up_backward.1 = (bf16[8,64,128]{2,1,0:T(8,128)(2,1)S(1)}, bf16[4,64,128]{2,1,0:T(8,128)(2,1)S(1)}, bf16[4,64,128]{2,1,0:T(8,128)(2,1)S(1)}, bf16[64,6144]{1,0:T...) custom-call(s32[4,48,128]{2,1,0:T(8,128)S(1)} %get-tuple-element.120.index_ref, ...), custom_call_target="tpu_custom_call" | custom-call | tf_op jit(solution)/shard_map/up_backward/pallas_call | solution.py:661
  71.4 6.7 %collective-permute-start.16 = (bf16[4,64,128]{2,1,0:T(8,128)(2,1)S(1)}, bf16[4,64,128]{2,1,0:T(8,128)(2,1)S(1)}, u32[]{:S(2)}, u32[]{:S(2)}) collective-permute-start(bf16[4,64,128]{2,1,0:T(8,128)(2,1)S(1)} %get-tuple-element.206), channel_id=1, source_target_pairs={{0,16},{4,68},{8,24},{12,76},{16,0},{20,84},{24,8},{28,92},{32,48}... | collective-permute-start | bytes 196616 | tf_op jit(solution)/shard_map/ppermute | solution.py:711
  78.8 2.1 %collective-permute-start.18 = (bf16[4,64,128]{2,1,0:T(8,128)(2,1)S(1)}, bf16[4,64,128]{2,1,0:T(8,128)(2,1)S(1)}, u32[]{:S(2)}, u32[]{:S(2)}) collective-permute-start(bf16[4,64,128]{2,1,0:T(8,128)(2,1)S(1)} %get-tuple-element.206), channel_id=1, source_target_pairs={{0,24},{4,100},{8,0},{12,108},{16,8},{20,116},{24,16},{28,124},{32... | collective-permute-start | bytes 196616 | tf_op jit(solution)/shard_map/ppermute | solution.py:711
  80.9 2.4 %collective-permute-start.19 = (bf16[4,64,128]{2,1,0:T(8,128)(2,1)S(1)}, bf16[4,64,128]{2,1,0:T(8,128)(2,1)S(1)}, u32[]{:S(2)}, u32[]{:S(2)}) collective-permute-start(bf16[4,64,128]{2,1,0:T(8,128)(2,1)S(1)} %get-tuple-element.185), channel_id=1, source_target_pairs={{4,8},{12,16},{20,24},{28,32},{36,40},{44,48},{52,56},{60,64},{68,... | collective-permute-start | bytes 196616 | tf_op jit(solution)/shard_map/ppermute | solution.py:682
  83.3 1.6 %feat_grad_up.1 = f32[64,6144]{1,0:T(8,128)} custom-call(bf16[64,6144]{1,0:T(8,128)(2,1)S(1)} %get-tuple-element.186.first_ref, bf16[2,64,192]{2,1,0:T(8,128)(2,1)S(1)} %get-tuple-element.122.w1_ref, bf16[8,64,128]{2,1,0:T(8,128)(2,1)S(1)} %collective-permute-done.15.rest_0_.h0), custom_call_target="tpu_custom_call" | custom-call | tf_op jit(solution)/shard_map/feat_grad_up/pallas_call | solution.py:661
  86.5 1.9 %collective-permute-start.20 = (bf16[7,64,128]{2,1,0:T(8,128)(2,1)S(1)}, bf16[7,64,128]{2,1,0:T(8,128)(2,1)S(1)}, u32[]{:S(2)}, u32[]{:S(2)}) collective-permute-start(bf16[7,64,128]{2,1,0:T(8,128)(2,1)S(1)} %get-tuple-element.215), channel_id=1, source_target_pairs={{0,3},{1,0},{2,1},{3,2},{4,7},{5,4},{6,5},{7,6},{8,11},{9,8},{10,9... | collective-permute-start | bytes 344072 | tf_op jit(solution)/shard_map/ppermute | solution.py:687
  89.1 3.5 %down_targets.1.start_ref = f32[64,3072]{1,0:T(8,128)S(1)} custom-call(s32[4,48,128]{2,1,0:T(8,128)S(1)} %get-tuple-element.141.index_ref, bf16[64,6144]{1,0:T(8,128)(2,1)S(1)} %get-tuple-element.159.first_ref, f32[64,3072]{1,0:T(8,128)S(1)} %bitcast.23, bf16[256,768]{1,0:T(8,128)(2,1)S(1)} %get-tuple-element.165.table, ...), custom_call_target="tpu_custom_call" | custom-call | tf_op jit(solution)/shard_map/down_targets/pallas_call | solution.py:661
  94.8 2.1 %collective-permute-start.23 = (bf16[4,64,128]{2,1,0:T(8,128)(2,1)S(1)}, bf16[4,64,128]{2,1,0:T(8,128)(2,1)S(1)}, u32[]{:S(2)}, u32[]{:S(2)}) collective-permute-start(bf16[4,64,128]{2,1,0:T(8,128)(2,1)S(1)} %fusion), channel_id=1, source_target_pairs={{0,64},{4,20},{8,72},{12,28},{16,80},{20,4},{24,88},{28,12},{32,96... | collective-permute-start | bytes 196616 | tf_op jit(solution)/shard_map/ppermute | solution.py:711
  96.9 2.9 %collective-permute-start.24 = (bf16[4,64,128]{2,1,0:T(8,128)(2,1)S(1)}, bf16[4,64,128]{2,1,0:T(8,128)(2,1)S(1)}, u32[]{:S(2)}, u32[]{:S(2)}) collective-permute-start(bf16[4,64,128]{2,1,0:T(8,128)(2,1)S(1)} %fusion), channel_id=1, source_target_pairs={{0,32},{4,12},{8,40},{12,20},{16,48},{20,28},{24,56},{28,4},{32,64... | collective-permute-start | bytes 196616 | tf_op jit(solution)/shard_map/ppermute | solution.py:711
  99.8 1.7 %lower_grad.1 = f32[64,3072]{1,0:T(8,128)} custom-call(bf16[8,64,128]{2,1,0:T(8,128)(2,1)S(1)} %collective-permute-done.15.rest_0_.h0, bf16[4,64,128]{2,1,0:T(8,128)(2,1)S(1)} %collective-permute-done.19.h1, bf16[4,64,128]{2,1,0:T(8,128)(2,1)S(1)} %get-tuple-element.189.h2, bf16[7,64,128]{2,1,0:T(8,128)(2,1)S(1)} %collective-permute-done.20.h3, ...), custom_call_target="tpu_custom_call" | custom-call | tf_op jit(solution)/shard_map/lower_grad/pallas_call | solution.py:661
  103.0 2.5 %collective-permute-start.26 = (bf16[4,64,128]{2,1,0:T(8,128)(2,1)S(1)}, bf16[4,64,128]{2,1,0:T(8,128)(2,1)S(1)}, u32[]{:S(2)}, u32[]{:S(2)}) collective-permute-start(bf16[4,64,128]{2,1,0:T(8,128)(2,1)S(1)} %reduce-precision_convert_fusion.own_ref), channel_id=1, source_target_pairs={{0,4},{4,0},{8,12},{12,8},{16,20},{20,16},{24,28},{28,24},{32,36},... | collective-permute-start | bytes 196616 | tf_op jit(solution)/shard_map/ppermute | solution.py:676
  (73 shorter events, 24.3 us)
Async XLA Ops:
  2.6 5.8 %collective-permute-start = (bf16[4,64,128]{2,1,0:T(8,128)(2,1)S(1)}, bf16[4,64,128]{2,1,0:T(8,128)(2,1)S(1)}, u32[]{:S(2)}, u32[]{:S(2)}) collective-permute-start(bf16[4,64,128]{2,1,0:T(8,128)(2,1)S(1)} %get-tuple-element.109), channel_id=1, source_target_pairs={{0,4},{4,0},{8,12},{12,8},{16,20},{20,16},{24,28},{28,24},{32,36},... | collective-permute-start | bytes 196616 | tf_op jit(solution)/shard_map/ppermute | solution.py:676
  4.1 5.6 %collective-permute-start.1 = (bf16[4,64,128]{2,1,0:T(8,128)(2,1)S(1)}, bf16[4,64,128]{2,1,0:T(8,128)(2,1)S(1)}, u32[]{:S(2)}, u32[]{:S(2)}) collective-permute-start(bf16[4,64,128]{2,1,0:T(8,128)(2,1)S(1)} %get-tuple-element.110), channel_id=1, source_target_pairs={{4,8},{12,16},{20,24},{28,32},{36,40},{44,48},{52,56},{60,64},{68,... | collective-permute-start | bytes 196616 | tf_op jit(solution)/shard_map/ppermute | solution.py:682
  9.7 5.6 %collective-permute-start.4 = (bf16[3,64,128]{2,1,0:T(8,128)(2,1)S(1)}, bf16[3,64,128]{2,1,0:T(8,128)(2,1)S(1)}, u32[]{:S(2)}, u32[]{:S(2)}) collective-permute-start(bf16[3,64,128]{2,1,0:T(8,128)(2,1)S(1)} %pad_maximum_fusion.5), channel_id=1, source_target_pairs={{0,3},{1,0},{2,1},{3,2},{4,7},{5,4},{6,5},{7,6},{8,11},{9,8},{10,9... | collective-permute-start | bytes 147464 | tf_op jit(solution)/shard_map/ppermute | solution.py:687
  12.6 4.6 %collective-permute-start.3 = (bf16[3,64,128]{2,1,0:T(8,128)(2,1)S(1)}, bf16[3,64,128]{2,1,0:T(8,128)(2,1)S(1)}, u32[]{:S(2)}, u32[]{:S(2)}) collective-permute-start(bf16[3,64,128]{2,1,0:T(8,128)(2,1)S(1)} %pad_maximum_fusion.4), channel_id=1, source_target_pairs={{0,2},{1,3},{2,0},{3,1},{4,6},{5,7},{6,4},{7,5},{8,10},{9,11},{10,... | collective-permute-start | bytes 147464 | tf_op jit(solution)/shard_map/ppermute | solution.py:687
  13.1 4.6 %collective-permute-start.2 = (bf16[3,64,128]{2,1,0:T(8,128)(2,1)S(1)}, bf16[3,64,128]{2,1,0:T(8,128)(2,1)S(1)}, u32[]{:S(2)}, u32[]{:S(2)}) collective-permute-start(bf16[3,64,128]{2,1,0:T(8,128)(2,1)S(1)} %pad_maximum_fusion.3), channel_id=1, source_target_pairs={{0,1},{1,2},{2,3},{3,0},{4,5},{5,6},{6,7},{7,4},{8,9},{9,10},{10,1... | collective-permute-start | bytes 147464 | tf_op jit(solution)/shard_map/ppermute | solution.py:687
  22.9 4.7 %collective-permute-start.5 = (bf16[4,64,128]{2,1,0:T(8,128)(2,1)S(1)}, bf16[4,64,128]{2,1,0:T(8,128)(2,1)S(1)}, u32[]{:S(2)}, u32[]{:S(2)}) collective-permute-start(bf16[4,64,128]{2,1,0:T(8,128)(2,1)S(1)} %get-tuple-element.138), channel_id=1, source_target_pairs={{0,4},{4,8},{8,12},{12,16},{16,20},{20,24},{24,28},{28,32},{32,36}... | collective-permute-start | bytes 196616 | tf_op jit(solution)/shard_map/ppermute | solution.py:692
  26.2 3.7 %collective-permute-start.6 = (bf16[4,64,128]{2,1,0:T(8,128)(2,1)S(1)}, bf16[4,64,128]{2,1,0:T(8,128)(2,1)S(1)}, u32[]{:S(2)}, u32[]{:S(2)}) collective-permute-start(bf16[4,64,128]{2,1,0:T(8,128)(2,1)S(1)} %get-tuple-element.139), channel_id=1, source_target_pairs={{0,124},{4,0},{8,4},{12,8},{16,12},{20,16},{24,20},{28,24},{32,28}... | collective-permute-start | bytes 196616 | tf_op jit(solution)/shard_map/ppermute | solution.py:692
  29.9 5.6 %collective-permute-start.9 = (bf16[3,64,128]{2,1,0:T(8,128)(2,1)S(1)}, bf16[3,64,128]{2,1,0:T(8,128)(2,1)S(1)}, u32[]{:S(2)}, u32[]{:S(2)}) collective-permute-start(bf16[3,64,128]{2,1,0:T(8,128)(2,1)S(1)} %pad_maximum_fusion.8), channel_id=1, source_target_pairs={{0,3},{1,0},{2,1},{3,2},{4,7},{5,4},{6,5},{7,6},{8,11},{9,8},{10,9... | collective-permute-start | bytes 147464 | tf_op jit(solution)/shard_map/ppermute | solution.py:687
  30.3 5.3 %collective-permute-start.8 = (bf16[3,64,128]{2,1,0:T(8,128)(2,1)S(1)}, bf16[3,64,128]{2,1,0:T(8,128)(2,1)S(1)}, u32[]{:S(2)}, u32[]{:S(2)}) collective-permute-start(bf16[3,64,128]{2,1,0:T(8,128)(2,1)S(1)} %pad_maximum_fusion.7), channel_id=1, source_target_pairs={{0,2},{1,3},{2,0},{3,1},{4,6},{5,7},{6,4},{7,5},{8,10},{9,11},{10,... | collective-permute-start | bytes 147464 | tf_op jit(solution)/shard_map/ppermute | solution.py:687
  31.1 4.6 %collective-permute-start.7 = (bf16[3,64,128]{2,1,0:T(8,128)(2,1)S(1)}, bf16[3,64,128]{2,1,0:T(8,128)(2,1)S(1)}, u32[]{:S(2)}, u32[]{:S(2)}) collective-permute-start(bf16[3,64,128]{2,1,0:T(8,128)(2,1)S(1)} %pad_maximum_fusion.6), channel_id=1, source_target_pairs={{0,1},{1,2},{2,3},{3,0},{4,5},{5,6},{6,7},{7,4},{8,9},{9,10},{10,1... | collective-permute-start | bytes 147464 | tf_op jit(solution)/shard_map/ppermute | solution.py:687
  48.0 3.7 %collective-permute-start.10 = (bf16[4,64,128]{2,1,0:T(8,128)(2,1)S(1)}, bf16[4,64,128]{2,1,0:T(8,128)(2,1)S(1)}, u32[]{:S(2)}, u32[]{:S(2)}) collective-permute-start(bf16[4,64,128]{2,1,0:T(8,128)(2,1)S(1)} %get-tuple-element.155), channel_id=1, source_target_pairs={{0,4},{4,8},{8,12},{12,16},{16,20},{20,24},{24,28},{28,32},{32,36}... | collective-permute-start | bytes 196616 | tf_op jit(solution)/shard_map/ppermute | solution.py:692
  50.4 3.7 %collective-permute-start.11 = (bf16[4,64,128]{2,1,0:T(8,128)(2,1)S(1)}, bf16[4,64,128]{2,1,0:T(8,128)(2,1)S(1)}, u32[]{:S(2)}, u32[]{:S(2)}) collective-permute-start(bf16[4,64,128]{2,1,0:T(8,128)(2,1)S(1)} %get-tuple-element.156), channel_id=1, source_target_pairs={{0,124},{4,0},{8,4},{12,8},{16,12},{20,16},{24,20},{28,24},{32,28}... | collective-permute-start | bytes 196616 | tf_op jit(solution)/shard_map/ppermute | solution.py:692
  54.1 7.6 %collective-permute-start.14 = (bf16[3,64,128]{2,1,0:T(8,128)(2,1)S(1)}, bf16[3,64,128]{2,1,0:T(8,128)(2,1)S(1)}, u32[]{:S(2)}, u32[]{:S(2)}) collective-permute-start(bf16[3,64,128]{2,1,0:T(8,128)(2,1)S(1)} %pad_maximum_fusion.11), channel_id=1, source_target_pairs={{0,1},{1,2},{2,3},{3,0},{4,5},{5,6},{6,7},{7,4},{8,9},{9,10},{10,1... | collective-permute-start | bytes 147464 | tf_op jit(solution)/shard_map/ppermute | solution.py:687
  54.2 7.4 %collective-permute-start.13 = (bf16[3,64,128]{2,1,0:T(8,128)(2,1)S(1)}, bf16[3,64,128]{2,1,0:T(8,128)(2,1)S(1)}, u32[]{:S(2)}, u32[]{:S(2)}) collective-permute-start(bf16[3,64,128]{2,1,0:T(8,128)(2,1)S(1)} %pad_maximum_fusion.10), channel_id=1, source_target_pairs={{0,2},{1,3},{2,0},{3,1},{4,6},{5,7},{6,4},{7,5},{8,10},{9,11},{10,... | collective-permute-start | bytes 147464 | tf_op jit(solution)/shard_map/ppermute | solution.py:687
  57.0 4.7 %collective-permute-start.12 = (bf16[3,64,128]{2,1,0:T(8,128)(2,1)S(1)}, bf16[3,64,128]{2,1,0:T(8,128)(2,1)S(1)}, u32[]{:S(2)}, u32[]{:S(2)}) collective-permute-start(bf16[3,64,128]{2,1,0:T(8,128)(2,1)S(1)} %pad_maximum_fusion.9), channel_id=1, source_target_pairs={{0,3},{1,0},{2,1},{3,2},{4,7},{5,4},{6,5},{7,6},{8,11},{9,8},{10,9... | collective-permute-start | bytes 147464 | tf_op jit(solution)/shard_map/ppermute | solution.py:687
  71.4 13.4 %collective-permute-start.16 = (bf16[4,64,128]{2,1,0:T(8,128)(2,1)S(1)}, bf16[4,64,128]{2,1,0:T(8,128)(2,1)S(1)}, u32[]{:S(2)}, u32[]{:S(2)}) collective-permute-start(bf16[4,64,128]{2,1,0:T(8,128)(2,1)S(1)} %get-tuple-element.206), channel_id=1, source_target_pairs={{0,16},{4,68},{8,24},{12,76},{16,0},{20,84},{24,8},{28,92},{32,48}... | collective-permute-start | bytes 196616 | tf_op jit(solution)/shard_map/ppermute | solution.py:711
  78.2 6.7 %collective-permute-start.17 = (bf16[4,64,128]{2,1,0:T(8,128)(2,1)S(1)}, bf16[4,64,128]{2,1,0:T(8,128)(2,1)S(1)}, u32[]{:S(2)}, u32[]{:S(2)}) collective-permute-start(bf16[4,64,128]{2,1,0:T(8,128)(2,1)S(1)} %get-tuple-element.206), channel_id=1, source_target_pairs={{0,8},{4,36},{8,16},{12,44},{16,24},{20,52},{24,0},{28,60},{32,40}... | collective-permute-start | bytes 196616 | tf_op jit(solution)/shard_map/ppermute | solution.py:711
  78.8 6.1 %collective-permute-start.18 = (bf16[4,64,128]{2,1,0:T(8,128)(2,1)S(1)}, bf16[4,64,128]{2,1,0:T(8,128)(2,1)S(1)}, u32[]{:S(2)}, u32[]{:S(2)}) collective-permute-start(bf16[4,64,128]{2,1,0:T(8,128)(2,1)S(1)} %get-tuple-element.206), channel_id=1, source_target_pairs={{0,24},{4,100},{8,0},{12,108},{16,8},{20,116},{24,16},{28,124},{32... | collective-permute-start | bytes 196616 | tf_op jit(solution)/shard_map/ppermute | solution.py:711
  80.9 5.6 %collective-permute-start.19 = (bf16[4,64,128]{2,1,0:T(8,128)(2,1)S(1)}, bf16[4,64,128]{2,1,0:T(8,128)(2,1)S(1)}, u32[]{:S(2)}, u32[]{:S(2)}) collective-permute-start(bf16[4,64,128]{2,1,0:T(8,128)(2,1)S(1)} %get-tuple-element.185), channel_id=1, source_target_pairs={{4,8},{12,16},{20,24},{28,32},{36,40},{44,48},{52,56},{60,64},{68,... | collective-permute-start | bytes 196616 | tf_op jit(solution)/shard_map/ppermute | solution.py:682
  86.5 6.1 %collective-permute-start.20 = (bf16[7,64,128]{2,1,0:T(8,128)(2,1)S(1)}, bf16[7,64,128]{2,1,0:T(8,128)(2,1)S(1)}, u32[]{:S(2)}, u32[]{:S(2)}) collective-permute-start(bf16[7,64,128]{2,1,0:T(8,128)(2,1)S(1)} %get-tuple-element.215), channel_id=1, source_target_pairs={{0,3},{1,0},{2,1},{3,2},{4,7},{5,4},{6,5},{7,6},{8,11},{9,8},{10,9... | collective-permute-start | bytes 344072 | tf_op jit(solution)/shard_map/ppermute | solution.py:687
  88.5 5.3 %collective-permute-start.21 = (bf16[7,64,128]{2,1,0:T(8,128)(2,1)S(1)}, bf16[7,64,128]{2,1,0:T(8,128)(2,1)S(1)}, u32[]{:S(2)}, u32[]{:S(2)}) collective-permute-start(bf16[7,64,128]{2,1,0:T(8,128)(2,1)S(1)} %get-tuple-element.214), channel_id=1, source_target_pairs={{0,2},{1,3},{2,0},{3,1},{4,6},{5,7},{6,4},{7,5},{8,10},{9,11},{10,... | collective-permute-start | bytes 344072 | tf_op jit(solution)/shard_map/ppermute | solution.py:687
  88.5 6.3 %collective-permute-start.22 = (bf16[7,64,128]{2,1,0:T(8,128)(2,1)S(1)}, bf16[7,64,128]{2,1,0:T(8,128)(2,1)S(1)}, u32[]{:S(2)}, u32[]{:S(2)}) collective-permute-start(bf16[7,64,128]{2,1,0:T(8,128)(2,1)S(1)} %get-tuple-element.213), channel_id=1, source_target_pairs={{0,1},{1,2},{2,3},{3,0},{4,5},{5,6},{6,7},{7,4},{8,9},{9,10},{10,1... | collective-permute-start | bytes 344072 | tf_op jit(solution)/shard_map/ppermute | solution.py:687
  94.8 6.7 %collective-permute-start.23 = (bf16[4,64,128]{2,1,0:T(8,128)(2,1)S(1)}, bf16[4,64,128]{2,1,0:T(8,128)(2,1)S(1)}, u32[]{:S(2)}, u32[]{:S(2)}) collective-permute-start(bf16[4,64,128]{2,1,0:T(8,128)(2,1)S(1)} %fusion), channel_id=1, source_target_pairs={{0,64},{4,20},{8,72},{12,28},{16,80},{20,4},{24,88},{28,12},{32,96... | collective-permute-start | bytes 196616 | tf_op jit(solution)/shard_map/ppermute | solution.py:711
  96.9 4.6 %collective-permute-start.24 = (bf16[4,64,128]{2,1,0:T(8,128)(2,1)S(1)}, bf16[4,64,128]{2,1,0:T(8,128)(2,1)S(1)}, u32[]{:S(2)}, u32[]{:S(2)}) collective-permute-start(bf16[4,64,128]{2,1,0:T(8,128)(2,1)S(1)} %fusion), channel_id=1, source_target_pairs={{0,32},{4,12},{8,40},{12,20},{16,48},{20,28},{24,56},{28,4},{32,64... | collective-permute-start | bytes 196616 | tf_op jit(solution)/shard_map/ppermute | solution.py:711
  (5 other events, 24.8 us)
where the time goes:
time: 107 us
  starting transfers between devices  44.8 us (42%)
  Pallas kernels  43 us (40%)
  waiting for transfers between devices  18.1 us (17%)
    pallas_call x12, Pallas kernels, run(): pl.pallas_call(kernel, name=name, grid=(steps,) if streamed else (), in_s...  43 us
    ppermute x6, starting transfers between devices, chip_ring(): return lax.ppermute(block, 'band', pairs)  14.4 us
    ppermute x12, starting transfers between devices, along_level(): lax.ppermute(block, 'level', [(i, (i + step) % count) for i in range(coun...  13.4 us
    ppermute x4, waiting for transfers between devices, along_band(): lax.ppermute(block, 'band', [(i, (i + step) % count) for i in range(count)])  7.36 us
    ppermute x2, starting transfers between devices, cross_swap(): lax.ppermute(block, 'band', pairs + [(b, a) for a, b in pairs] + [(0, 0),...  5.9 us
    ppermute x4, starting transfers between devices, along_band(): lax.ppermute(block, 'band', [(i, (i + step) % count) for i in range(count)])  5.68 us
    ppermute x3, starting transfers between devices, core_swap(): lax.ppermute(block, 'band', [(i, i ^ 1) for i in range(lax.axis_size('ban...  5.4 us
    ppermute x12, waiting for transfers between devices, along_level(): lax.ppermute(block, 'level', [(i, (i + step) % count) for i in range(coun...  4.62 us
  transfers between devices with their start and end apart: 27, of which 14 were waited for; matrix products, arithmetic and copies ran while one was open for 0% of the time, Pallas kernels for 14%

commit v1 on v0

--- a/solution.py
+++ b/solution.py
@@ -82,7 +82,7 @@
 def row_of(ref, k, start, size):
     rows = size // 128
     if not isinstance(start, int):
-        start = pl.multiple_of(start // 128, rows)
+        start = start // 128
         return jnp.concatenate([ref[k, pl.ds(start + r, 1), :] for r in range(rows)], axis=1)
     return jnp.concatenate([ref[k, r : r + 1, :] for r in range(start // 128, start // 128 + rows)], axis=1)
 
@@ -208,7 +208,7 @@
 
 
 def tables_kernel(upper_rows, lower_rows, counts_up, counts_down, senders_up, targets_up, senders_down, targets_down,
-                  index_up, alive_up, index_down, alive_down, limits_up, limits_down, sems):
+                  w1_ref, w2_ref, wn1_ref, wn2_ref, biases_ref, gains_ref, index_up, alive_up, index_down, alive_down, columns_ref, w1t_ref, w2t_ref, wn1t_ref, wn2t_ref, limits_up, limits_down, sems):
     copies = [pltpu.make_async_copy(counts_up, limits_up, sems.at[0]), pltpu.make_async_copy(counts_down, limits_down, sems.at[1])]
     for copy in copies:
         copy.start()
@@ -216,6 +216,10 @@
     for index_ref, senders_ref, targets_ref, rows, swapped in sweeps:
         index_ref[0], index_ref[1] = place(targets_ref[...], *groups_of(rows))
         index_ref[2], index_ref[3] = slot_place(senders_ref[...], swapped)
+    for k in range(2):
+        columns_ref[k] = columns_of(biases_ref, gains_ref, k)
+        for turned, ref in ((w1t_ref, w1_ref), (w2t_ref, w2_ref), (wn1t_ref, wn1_ref), (wn2t_ref, wn2_ref)):
+            turned[k] = transposed(ref[k])
     for copy in copies:
         copy.wait()
     alive_up[0] = live(senders_up[...], limits_up)
@@ -238,27 +242,29 @@
         copy.wait()
 
 
-def part_kernel(k, block, index_ref, feat_ref, local_ref, w1_ref, biases_ref, gains_ref, *rest):
+def part_kernel(k, block, first, index_ref, feat_ref, local_ref, w1_ref, columns_ref, *rest):
     part_ref, rows_ref, table, sem = rest[-4:]
-    copy = pltpu.make_async_copy(feat_ref, rows_ref.at[0:D], sem)
+    size = part_ref.shape[1]
+    copy = pltpu.make_async_copy(feat_ref.at[:, pl.ds(first, size)], rows_ref.at[0:D], sem)
     copy.start()
     groups, n = groups_of(local_ref.shape[1])
     pack_table(table, local_ref, groups, n)
-    columns = columns_of(biases_ref, gains_ref, k)
+    columns = columns_ref[k]
     weight = jnp.concatenate([w1_ref[k, :, 0:D], w1_ref[k, :, 2 * D : 3 * D]], axis=1)
 
     def body(s):
-        rows_ref[D : 2 * D, s] = pick(table, row_of(index_ref, 0, s.start, s.size), row_of(index_ref, 1, s.start, s.size), groups, n)
-
-    over_blocks(feat_ref.shape[1], block, body)
+        a = first + s.start
+        rows_ref[D : 2 * D, s] = pick(table, row_of(index_ref, 0, a, s.size), row_of(index_ref, 1, a, s.size), groups, n)
+
+    over_blocks(size, block, body)
     copy.wait()
     part_ref[...] = dot(weight, rows_ref[...]) + columns[:, 0:1]
 
 
-def edges_forward(k, parts, alive_ref, index_ref, table, w1_ref, w2_ref, columns, total, groups, n,
+def edges_forward(k, parts, alive_ref, index_ref, table, w1_ref, w2t_ref, columns, total, groups, n,
                   slope_ref, normed_ref, hidden_ref, factor_ref):
     weight_slot = w1_ref[k, :, D : 2 * D]
-    weight_two = w2_ref[k].astype(F32).T.astype(B16)
+    weight_two = w2t_ref[k]
     total[...] = jnp.zeros_like(total)
 
     def slot_rows(span, unused):
@@ -366,15 +372,15 @@
 
 
 def up_forward_kernel(part_ref, alive_ref, index_ref, r0, r1, r2, r3, r4, r5, local_ref, send_ref,
-                      w1_ref, w2_ref, wn1_ref, wn2_ref, biases_ref, gains_ref,
+                      w1_ref, w2t_ref, wn1_ref, wn2t_ref, columns_ref,
                       out_ref, summed_ref, s0, s1, s2, slope_ref, normed_ref, hidden_ref, factor_ref,
-                      slots, total, table, out, sem):
+                      node_hidden_ref, node_slope_ref, node_normed_ref, node_factor_ref, slots, total, table, out, sem):
     groups, n = groups_of(local_ref.shape[1])
-    columns = columns_of(biases_ref, gains_ref, 0)
+    columns = columns_ref[0]
     slot_table(slots, (r0, r1, r2, r3, r4, r5))
-    edges_forward(0, (part_ref,), alive_ref, index_ref, slots, w1_ref, w2_ref, columns, total, groups, n,
+    edges_forward(0, (part_ref,), alive_ref, index_ref, slots, w1_ref, w2t_ref, columns, total, groups, n,
                   slope_ref, normed_ref, hidden_ref, factor_ref)
-    weight_two = transposed(wn2_ref[0])
+    weight_two = wn2t_ref[0]
 
     def first_layer(j, unused):
         s = slice(j * n, (j + 1) * n)
@@ -384,7 +390,12 @@
 
     def second_layer(j, held):
         s = slice(j * n, (j + 1) * n)
-        normed, unused = node_second(held[0], weight_two, columns)
+        hidden, slope = held
+        normed, factor = node_second(hidden, weight_two, columns)
+        node_hidden_ref[:, s] = hidden
+        node_slope_ref[:, s] = slope
+        node_normed_ref[:, s] = normed
+        node_factor_ref[:, s] = factor
         result = local_ref[:, s].astype(F32) + normed * columns[:, 7:8] + columns[:, 5:6]
         out[:, s] = result
         table[j * D : (j + 1) * D, :] = result.astype(B16)
@@ -396,21 +407,21 @@
     copy.wait()
 
 
-def down_kernel(part_ref, alive_ref, index_ref, r0, r1, r2, r3, r4, r5, local_ref, cot_ref,
-                w1_ref, w2_ref, wn1_ref, wn2_ref, biases_ref, gains_ref,
+def down_kernel(part_a, part_b, alive_ref, index_ref, r0, r1, r2, r3, r4, r5, local_ref, cot_ref,
+                w1_ref, w1t_ref, w2_ref, w2t_ref, wn1_ref, wn1t_ref, wn2_ref, wn2t_ref, columns_ref,
                 out_ref, g0, g1, g2, first_ref, second_ref, hidden_ref, sums_ref, edge_sums, node_sums,
                 table, summed_ref, node_hidden_ref, node_second_ref,
                 slots, total, slope_ref, normed_ref, factor_ref, out, sem):
     groups, n = groups_of(local_ref.shape[1])
-    columns = columns_of(biases_ref, gains_ref, 1)
+    columns = columns_ref[1]
     slot_table(slots, (r0, r1, r2, r3, r4, r5))
-    parts = (part_ref,)
-    edges_forward(1, parts, alive_ref, index_ref, slots, w1_ref, w2_ref, columns, total, groups, n,
+    parts = (part_a, part_b)
+    edges_forward(1, parts, alive_ref, index_ref, slots, w1_ref, w2t_ref, columns, total, groups, n,
                   slope_ref, normed_ref, hidden_ref, factor_ref)
     clear((node_sums, edge_sums, sums_ref))
     wn2 = wn2_ref[1]
-    wn2_t = transposed(wn2)
-    wn1 = transposed(wn1_ref[1])
+    wn2_t = wn2t_ref[1]
+    wn1 = wn1t_ref[1]
 
     def first_layer(j, unused):
         summed = total[j * D : (j + 1) * D, :].astype(B16)
@@ -436,7 +447,7 @@
     copy = pltpu.make_async_copy(out, out_ref, sem)
     copy.start()
     weight_two = w2_ref[1]
-    weight_slot = transposed(w1_ref[1, :, D : 2 * D])
+    weight_slot = w1t_ref[1, D : 2 * D]
 
     def grad_rows(span, unused):
         a, size = span[2].start, span[2].size
@@ -461,10 +472,10 @@
     copy.wait()
 
 
-def down_targets_kernel(index_ref, first_ref, cot_ref, table, w1_ref, wn1_ref, *rest):
+def down_targets_kernel(index_ref, first_ref, cot_ref, table, w1t_ref, wn1t_ref, *rest):
     grad_ref, total = rest[-2:]
     groups, n = groups_of(cot_ref.shape[1])
-    weight = transposed(w1_ref[1, :, 2 * D : 3 * D])
+    weight = w1t_ref[1, 2 * D : 3 * D]
     total[...] = jnp.zeros_like(total)
 
     def body(s):
@@ -472,7 +483,7 @@
         add_at(total, first_ref[:, s], group, column, groups, n)
 
     over_blocks(first_ref.shape[1], EDGE_BLOCK, body)
-    weight_node = transposed(wn1_ref[1, :, 0:D])
+    weight_node = wn1t_ref[1, 0:D]
 
     def start(j):
         return cot_ref[:, j * n : (j + 1) * n] + dot(weight_node, table[j * D : (j + 1) * D, :])
@@ -480,11 +491,10 @@
     target_grads(total, weight, start, grad_ref, groups, n)
 
 
-def down_rest_kernel(rows_ref, first_ref, second_ref, hidden_ref, r0, r1, r2, r3, r4, r5, sums_ref, edge_in, node_in,
-                     table, summed_ref, node_hidden_ref, node_second_ref, local_ref, w1_ref, *rest):
-    feat_grad_ref, packed_ref, slots, one_ref, two_ref, wn1_grad, wn2_grad, edge_sums, node_sums = rest[-9:]
+def down_rest_kernel(rows_a, rows_b, first_ref, second_ref, hidden_ref, r0, r1, r2, r3, r4, r5, sums_ref, edge_in, node_in,
+                     table, summed_ref, node_hidden_ref, node_second_ref, local_ref, *rest):
+    packed_ref, slots, one_ref, two_ref, wn1_grad, wn2_grad, edge_sums, node_sums = rest[-8:]
     step = pl.program_id(0)
-    weight = transposed(w1_ref[1, :, 0:D])
 
     @pl.when(step == 0)
     def _():
@@ -494,8 +504,8 @@
 
     s = pl.ds(pl.multiple_of(step * EDGE_BLOCK, EDGE_BLOCK), EDGE_BLOCK)
     first = first_ref[:, s]
-    feat_grad_ref[...] = dot(weight, first)
-    edge_weight_grads(first, second_ref[:, s], rows_ref[:, s], hidden_ref[:, s], one_ref, two_ref, edge_sums)
+    rows = jnp.where(step == 0, rows_a[...], rows_b[...])
+    edge_weight_grads(first, second_ref[:, s], rows, hidden_ref[:, s], one_ref, two_ref, edge_sums)
 
     @pl.when(step == pl.num_programs(0) - 1)
     def _():
@@ -518,38 +528,33 @@
 
 def up_backward_kernel(index_ref, rows_ref, h0, h1, h2, h3, h4, h5,
                        send_ref, cot_ref, local_ref, summed_ref, r0, r1, r2, r3, r4, r5, slope_ref, normed_ref, hidden_ref, factor_ref, alive_ref, packed_down_ref,
-                       w1_ref, w2_ref, wn1_ref, wn2_ref, biases_ref, gains_ref,
+                       node_hidden_ref, node_slope_ref, node_normed_ref, node_factor_ref, w1t_ref, w2_ref, wn1t_ref, wn2_ref, columns_ref,
                        partner_ref, cross_ref, own_ref, first_ref, grad_ref, keep_ref,
                        slots, table, back, total, sums, start, one_ref, two_ref, edge_sums, node_sums, wn1_grad, wn2_grad, pieces):
     groups, n = groups_of(local_ref.shape[1])
-    columns = columns_of(biases_ref, gains_ref, 0)
+    columns = columns_ref[0]
     clear((back, total, sums, one_ref, two_ref, edge_sums, node_sums, wn1_grad, wn2_grad))
     slot_table(slots, (r0, r1, r2, r3, r4, r5))
     add_back(back, (h0, h1, h2, h3, h4, h5), send_ref, groups, n, False)
     wn2 = wn2_ref[0]
-    wn2_t = transposed(wn2)
-    wn1 = transposed(wn1_ref[0])
-    w1 = transposed(w1_ref[0])
-
-    def first_layer(j, unused):
+    wn1 = wn1t_ref[0]
+    w1 = w1t_ref[0]
+
+    def second_layer(j, unused):
+        s = slice(j * n, (j + 1) * n)
+        grad = cot_ref[:, s] + back[j * D : (j + 1) * D, :]
+        return grad, node_second_grad(grad, node_normed_ref[:, s], node_factor_ref[:, s], columns, node_sums)
+
+    def node_grads(j, held):
+        grad, second = held
         s = slice(j * n, (j + 1) * n)
         inputs = jnp.concatenate([local_ref[:, s], summed_ref[:, s]], axis=0)
-        return inputs, *node_first(0, inputs, wn1_ref, columns)
-
-    def second_layer(j, held):
-        inputs, hidden, slope = held
-        grad = cot_ref[:, j * n : (j + 1) * n] + back[j * D : (j + 1) * D, :]
-        normed, factor = node_second(hidden, wn2_t, columns)
-        return inputs, hidden, slope, grad, node_second_grad(grad, normed, factor, columns, node_sums)
-
-    def node_grads(j, held):
-        inputs, hidden, slope, grad, second = held
-        first = (dot(wn2, second) * slope).astype(B16)
-        node_weight_grads(first, second, inputs, hidden, wn1_grad, wn2_grad, node_sums)
+        first = (dot(wn2, second) * node_slope_ref[:, s]).astype(B16)
+        node_weight_grads(first, second, inputs, node_hidden_ref[:, s], wn1_grad, wn2_grad, node_sums)
         table[j * D : (j + 1) * D, :] = first
         start[:, j * n : (j + 1) * n] = grad + dot(wn1[0:D], first)
 
-    pipelined((first_layer, second_layer, node_grads), range(groups))
+    pipelined((second_layer, node_grads), range(groups))
     weight_two = w2_ref[0]
 
     def grad_rows(span, unused):
@@ -586,9 +591,10 @@
         partner_ref[4 + p] = pieces[(1 - core) * 4 + p].astype(B16)
 
 
-def feat_grad_kernel(first_ref, w1_ref, *rest):
-    out_ref = rest[-1]
-    out_ref[...] = dot(transposed(w1_ref[0, :, 0:D]), first_ref[...])
+def feat_grad_kernel(up_ref, down_ref, w1t_ref, *rest):
+    out_up, out_down = rest[-2:]
+    out_up[...] = dot(w1t_ref[0, 0:D], up_ref[...])
+    out_down[...] = dot(w1t_ref[1, 0:D], down_ref[...])
 
 
 def lower_grad_kernel(h0, h1, h2, h3, h4, h5, send_ref, start_ref, out_ref, total):
@@ -758,32 +764,36 @@
         [pltpu.VMEM(lower_table, B16), pltpu.SemaphoreType.DMA((count,))], 0, raw=range(count),
     )(*early)
     index, lives = shape((4, *dense), jnp.int32), shape((1, *dense))
-    index_up, alive_up, index_down, alive_down = call(
-        functools.partial(tables_kernel, upper_rows, lower_rows), "edge_tables", [index, lives, index, lives],
+    turned = [shape((2, D, 8)), shape((2, 3 * D, D), B16), shape((2, D, D), B16), shape((2, 2 * D, D), B16), shape((2, D, D), B16)]
+    index_up, alive_up, index_down, alive_down, columns, w1t, w2t, wn1t, wn2t = call(
+        functools.partial(tables_kernel, upper_rows, lower_rows), "edge_tables", [index, lives, index, lives] + turned,
         [pltpu.SMEM((1, 12), jnp.int32), pltpu.SMEM((1, 12), jnp.int32), pltpu.SemaphoreType.DMA((2,))], 0, raw=(0, 1),
-    )(up_counts, down_counts, senders_up, targets_up, senders_down, targets_down)
-
-    def part(k, block, name, table, index, feat, local, after):
+    )(up_counts, down_counts, senders_up, targets_up, senders_down, targets_down, w1, w2, wn1, wn2, bias_rows, norm_gains)
+
+    def part(k, block, first, size, name, table, index, feat, local, after):
         return call(
-            functools.partial(part_kernel, k, block), name, [wide32, shape((2 * D, edges), B16)],
+            functools.partial(part_kernel, k, block, first), name, [shape((D, size)), shape((2 * D, size), B16)],
             [pltpu.VMEM(table, B16), pltpu.SemaphoreType.DMA], 0, raw=(1,),
-        )(index, feat, local, w1, bias_rows, norm_gains, after=after)
+        )(index, feat, local, w1, columns, after=after)
 
     sent = [core_swap(sent[0]), cross_swap(sent[1]), sent[2]]
-    sent, alive_up = lax.optimization_barrier((sent, alive_up))
-    part_up, rows_up = part(0, EDGE_BLOCK, "part_up", upper_table, index_up, feat_up, upper, (sent[0], sent[1]))
+    half = edges // 2
+    part_a, rows_a = part(1, half // 2, 0, half, "part_down_a", lower_table, index_down, feat_down, lower, ())
+    sent, part_a = lax.optimization_barrier((sent, part_a))
+    part_up, rows_up = part(0, EDGE_BLOCK, 0, edges, "part_up", upper_table, index_up, feat_up, upper, (sent[0], sent[1]))
     up_slots = along_levels(sent, 1)
     up_slots, part_up = lax.optimization_barrier((up_slots, part_up))
-    (upper_new, summed_up, s0, s1, s2, slope, normed, hidden, factor) = call(
+    (upper_new, summed_up, s0, s1, s2, slope, normed, hidden, factor, *nodes_up) = call(
         up_forward_kernel, "up_forward",
-        [shape((D, upper_rows)), shape((D, upper_rows), B16)] + [block] * 3 + [wide32, wide32, wide16, row],
+        [shape((D, upper_rows)), shape((D, upper_rows), B16)] + [block] * 3 + [wide32, wide32, wide16, row,
+         shape((D, upper_rows), B16), shape((D, upper_rows)), shape((D, upper_rows)), shape((1, upper_rows))],
         [slots, pltpu.VMEM(upper_table, F32), pltpu.VMEM(upper_table, B16), pltpu.VMEM((D, upper_rows), F32),
          pltpu.SemaphoreType.DMA], 0, (0,),
-    )(part_up, alive_up, index_up, *up_slots, upper, down_send, w1, w2, wn1, wn2, bias_rows, norm_gains)
+    )(part_up, alive_up, index_up, *up_slots, upper, down_send, w1, w2t, wn1, wn2t, columns)
     sent = across_bands([s0, s1, s2])
-    part_down, rows_down = part(1, EDGE_BLOCK, "part_down", lower_table, index_down, feat_down, lower, (sent[0], sent[1]))
+    part_b, rows_b = part(1, half // 2, half, half, "part_down_b", lower_table, index_down, feat_down, lower, (sent[0], sent[1]))
     down_slots = along_levels(sent, 1)
-    down_slots, part_down = lax.optimization_barrier((down_slots, part_down))
+    down_slots, part_b = lax.optimization_barrier((down_slots, part_b))
     sums_shape = shape((SLOT_GROUPS * D, SLOT_COLS))
     node16 = shape((D, lower_rows), B16)
     (lower_new, g0, g1, g2, first_down, second_down, hidden_down, sums_down, edge_sums, node_sums, *nodes) = call(
@@ -793,13 +803,13 @@
         [slots, pltpu.VMEM(lower_table, F32), pltpu.VMEM((D, edges), F32),
          pltpu.VMEM((D, edges), F32), pltpu.VMEM((1, edges), F32),
          pltpu.VMEM((D, lower_rows), F32), pltpu.SemaphoreType.DMA], 0, (0,),
-    )(part_down, alive_down, index_down, *down_slots, lower, cot_lower, w1, w2, wn1, wn2, bias_rows, norm_gains)
+    )(part_a, part_b, alive_down, index_down, *down_slots, lower, cot_lower, w1, w1t, w2, w2t, wn1, wn1t, wn2, wn2t, columns)
     back = across_bands([g0, g1, g2])
-    feat_grad_down, packed_down = call(
-        down_rest_kernel, "down_rest", [wide32, four],
+    (packed_down,) = call(
+        down_rest_kernel, "down_rest", [four],
         [slots, pltpu.VMEM((D, 2 * D), F32), pltpu.VMEM((D, D), F32), pltpu.VMEM((D, 2 * D), F32), pltpu.VMEM((D, D), F32),
-         pltpu.VMEM((4, D, 128), F32), pltpu.VMEM((4, D, 128), F32)], 0, (), (steps, (), (0,)),
-    )(rows_down, first_down, second_down, hidden_down, *down_slots, sums_down, edge_sums, node_sums, *nodes, lower, w1,
+         pltpu.VMEM((4, D, 128), F32), pltpu.VMEM((4, D, 128), F32)], 0, (), (steps, (), ()),
+    )(rows_a, rows_b, first_down, second_down, hidden_down, *down_slots, sums_down, edge_sums, node_sums, *nodes, lower,
       after=(back[0], back[1]))
     down_back = along_levels(back, -1)
     down_back, packed_down = lax.optimization_barrier((down_back, packed_down))
@@ -811,15 +821,16 @@
          pltpu.VMEM((D, 2 * D), F32), pltpu.VMEM((D, D), F32), pltpu.VMEM((4, D, 128), F32), pltpu.VMEM((4, D, 128), F32),
          pltpu.VMEM((D, 2 * D), F32), pltpu.VMEM((D, D), F32), pltpu.VMEM((8, D, 128), F32)], 0, (), None, (4,),
     )(index_up, rows_up, *down_back, down_send, cot_upper, upper, summed_up, *up_slots,
-      slope, normed, hidden, factor, alive_up, packed_down, w1, w2, wn1, wn2, bias_rows, norm_gains)
+      slope, normed, hidden, factor, alive_up, packed_down, *nodes_up, w1t, w2, wn1t, wn2, columns)
 
     partner = core_swap(partner)
     total = rounded(rounded(keep) + partner[4:].astype(F32))
     cross, keep = lax.optimization_barrier((cross, total))
     cross = cross_swap(cross)
     total = sum_along(total, (2, 8))
-    (feat_grad_up,) = call(feat_grad_kernel, "feat_grad_up", [wide32], [], 0, (), (steps, (0,), (0,)))(
-        first_up, w1, after=(partner,))
+    feat_grad_up, feat_grad_down = call(
+        feat_grad_kernel, "feat_grads", [wide32, wide32], [], 0, (), (steps, (0, 1), (0, 1)),
+    )(first_up, first_down, w1t, after=(partner,))
     total, cross, feat_grad_up = lax.optimization_barrier((total, cross, feat_grad_up))
     blocks = (partner, cross, own)
     total = rounded(total)
@@ -828,7 +839,7 @@
     ]
     (start_lower,) = call(
         down_targets_kernel, "down_targets", [shape((D, lower_rows))], [pltpu.VMEM(lower_table, F32)],
-    )(index_down, first_down, cot_lower, nodes[0], w1, wn1, after=(total,))
+    )(index_down, first_down, cot_lower, nodes[0], w1t, wn1t, after=(total,))
     levels, start_lower = lax.optimization_barrier((levels, start_lower))
     total = sum_of_four(total, *(b[3:] for b in levels))
     (grad_lower,) = call(lower_grad_kernel, "lower_grad", [shape((D, lower_rows))], [pltpu.VMEM(lower_table, F32)], 0, (), None, (0,))(

time: 107 us -> 106 us (level)
  waiting for transfers between devices: 18.1 us -> 16.6 us
  starting transfers between devices: 44.8 us -> 45.9 us
    ppermute x6, starting transfers between devices: 14.4 us -> 10.6 us  [chip_ring(): return lax.ppermute(block, 'band', pairs)]
    ppermute x2, waiting for transfers between devices: 2.8 us -> 0.01 us  [cross_swap(): lax.ppermute(block, 'band', pairs + [(b, a) for a, b in pairs] + [(0, 0),...]
    ppermute x3, starting transfers between devices: 5.4 us -> 7.44 us  [core_swap(): lax.ppermute(block, 'band', [(i, i ^ 1) for i in range(lax.axis_size('ban...]
    ppermute x12, starting transfers between devices: 13.4 us -> 15.4 us  [along_level(): lax.ppermute(block, 'level', [(i, (i + step) % count) for i in range(coun...]
    ppermute x2, starting transfers between devices: 5.9 us -> 7.6 us  [cross_swap(): lax.ppermute(block, 'band', pairs + [(b, a) for a, b in pairs] + [(0, 0),...]
    pallas_call x12 -> x13, Pallas kernels: 43 us -> 42.5 us  [run(): pl.pallas_call(kernel, name=name, grid=(steps,) if streamed else (), in_s...]
where the time goes in v1:
time: 106 us
  starting transfers between devices  45.9 us (43%)
  Pallas kernels  42.5 us (40%)
  waiting for transfers between devices  16.6 us (16%)
    pallas_call x13, Pallas kernels, run(): pl.pallas_call(kernel, name=name, grid=(steps,) if streamed else (), in_s...  42.5 us
    ppermute x12, starting transfers between devices, along_level(): lax.ppermute(block, 'level', [(i, (i + step) % count) for i in range(coun...  15.4 us
    ppermute x6, starting transfers between devices, chip_ring(): return lax.ppermute(block, 'band', pairs)  10.6 us
    ppermute x2, starting transfers between devices, cross_swap(): lax.ppermute(block, 'band', pairs + [(b, a) for a, b in pairs] + [(0, 0),...  7.6 us
    ppermute x3, starting transfers between devices, core_swap(): lax.ppermute(block, 'band', [(i, i ^ 1) for i in range(lax.axis_size('ban...  7.44 us
    ppermute x4, waiting for transfers between devices, along_band(): lax.ppermute(block, 'band', [(i, (i + step) % count) for i in range(count)])  7.37 us
    ppermute x12, waiting for transfers between devices, along_level(): lax.ppermute(block, 'level', [(i, (i + step) % count) for i in range(coun...  5.24 us
    ppermute x4, starting transfers between devices, along_band(): lax.ppermute(block, 'band', [(i, (i + step) % count) for i in range(count)])  4.82 us
  transfers between devices with their start and end apart: 27, of which 14 were waited for; matrix products, arithmetic and copies ran while one was open for 0% of the time, Pallas kernels for 14%

profile of v1, /device:TPU:1, one launch (start us, length us, event | category | flops | bytes accessed | tf_op | source)
XLA Modules:
  0.0 106.3 jit_solution(1786917611733651445)
XLA Ops:
  0.7 2.0 %send_lower.1 = (bf16[4,64,128]{2,1,0:T(8,128)(2,1)S(1)}, bf16[4,64,128]{2,1,0:T(8,128)(2,1)S(1)}, bf16[4,64,128]{2,1,0:T(8,128)(2,1)S(1)}, s32[12,128]{1,0:T(8,...) custom-call(s32[12,128]{1,0:T(8,128)} %refs_0_.1, ...), custom_call_target="tpu_custom_call" | custom-call | tf_op jit(solution)/shard_map/send_lower/pallas_call | solution.py:667
  4.1 3.5 %collective-permute-start.1 = (bf16[4,64,128]{2,1,0:T(8,128)(2,1)S(1)}, bf16[4,64,128]{2,1,0:T(8,128)(2,1)S(1)}, u32[]{:S(2)}, u32[]{:S(2)}) collective-permute-start(bf16[4,64,128]{2,1,0:T(8,128)(2,1)S(1)} %get-tuple-element.121), channel_id=1, source_target_pairs={{4,8},{12,16},{20,24},{28,32},{36,40},{44,48},{52,56},{60,64},{68,... | collective-permute-start | bytes 196616 | tf_op jit(solution)/shard_map/ppermute | solution.py:688
  8.5 1.9 %part_down_a.1 = (f32[64,3072]{1,0:T(8,128)S(1)}, bf16[128,3072]{1,0:T(8,128)(2,1)S(1)}) custom-call(s32[4,48,128]{2,1,0:T(8,128)S(1)} %get-tuple-element.133.index_ref, bf16[64,6144]{1,0:T(8,128)(2,1)} %bitcast.25, bf16[64,3072]{1,0:T(8,128)(2,1)S(1)} %get-tuple-element.134.local_ref, bf16[2,64,192]{2,1,0:T(8,128)(2,1)S(1)} %get-tuple-element.127.w1_ref, ...), custom_call_target="tpu_custom_call" | custom-call | tf_op jit(solution)/shard_map/part_down_a/pallas_call | solution.py:667
  11.9 2.7 %collective-permute-start.3 = (bf16[3,64,128]{2,1,0:T(8,128)(2,1)S(1)}, bf16[3,64,128]{2,1,0:T(8,128)(2,1)S(1)}, u32[]{:S(2)}, u32[]{:S(2)}) collective-permute-start(bf16[3,64,128]{2,1,0:T(8,128)(2,1)S(1)} %pad_maximum_fusion.4), channel_id=1, source_target_pairs={{0,2},{1,3},{2,0},{3,1},{4,6},{5,7},{6,4},{7,5},{8,10},{9,11},{10,... | collective-permute-start | bytes 147464 | tf_op jit(solution)/shard_map/ppermute | solution.py:693
  17.6 5.2 %up_forward.1 = (f32[64,768]{1,0:T(8,128)}, bf16[64,768]{1,0:T(8,128)(2,1)S(1)}, bf16[4,64,128]{2,1,0:T(8,128)(2,1)S(1)}, bf16[4,64,128]{2,1,0:T(8,128)(2,1)S(1)...) custom-call(f32[64,6144]{1,0:T(8,128)S(1)} %get-tuple-element.144.pa, ...), custom_call_target="tpu_custom_call" | custom-call | tf_op jit(solution)/shard_map/up_forward/pallas_call | solution.py:667
  22.8 2.8 %collective-permute-start.5 = (bf16[4,64,128]{2,1,0:T(8,128)(2,1)S(1)}, bf16[4,64,128]{2,1,0:T(8,128)(2,1)S(1)}, u32[]{:S(2)}, u32[]{:S(2)}) collective-permute-start(bf16[4,64,128]{2,1,0:T(8,128)(2,1)S(1)} %get-tuple-element.155), channel_id=1, source_target_pairs={{0,4},{4,8},{8,12},{12,16},{16,20},{20,24},{24,28},{28,32},{32,36}... | collective-permute-start | bytes 196616 | tf_op jit(solution)/shard_map/ppermute | solution.py:698
  27.0 2.4 %collective-permute-done.6.rest_1_.r1 = bf16[4,64,128]{2,1,0:T(8,128)(2,1)S(1)} collective-permute-done((bf16[4,64,128]{2,1,0:T(8,128)(2,1)S(1)}, bf16[4,64,128]{2,1,0:T(8,128)(2,1)S(1)}, u32[]{:S(2)}, u32[]{:S(2)}) %collective-permute-start.6) | collective-permute-done | bytes 65568 | tf_op jit(solution)/shard_map/ppermute | solution.py:698
  29.9 3.1 %collective-permute-start.8 = (bf16[3,64,128]{2,1,0:T(8,128)(2,1)S(1)}, bf16[3,64,128]{2,1,0:T(8,128)(2,1)S(1)}, u32[]{:S(2)}, u32[]{:S(2)}) collective-permute-start(bf16[3,64,128]{2,1,0:T(8,128)(2,1)S(1)} %pad_maximum_fusion.7), channel_id=1, source_target_pairs={{0,2},{1,3},{2,0},{3,1},{4,6},{5,7},{6,4},{7,5},{8,10},{9,11},{10,... | collective-permute-start | bytes 147464 | tf_op jit(solution)/shard_map/ppermute | solution.py:693
  33.6 1.9 %part_down_b.1 = (f32[64,3072]{1,0:T(8,128)S(1)}, bf16[128,3072]{1,0:T(8,128)(2,1)S(1)}) custom-call(s32[4,48,128]{2,1,0:T(8,128)S(1)} %get-tuple-element.133.index_ref, bf16[64,6144]{1,0:T(8,128)(2,1)} %bitcast.26, bf16[64,3072]{1,0:T(8,128)(2,1)S(1)} %get-tuple-element.134.local_ref, bf16[2,64,192]{2,1,0:T(8,128)(2,1)S(1)} %get-tuple-element.127.w1_ref, ...), custom_call_target="tpu_custom_call" | custom-call | tf_op jit(solution)/shard_map/part_down_b/pallas_call | solution.py:667
  36.2 12.3 %down_sweep.1 = (f32[64,3072]{1,0:T(8,128)}, bf16[4,64,128]{2,1,0:T(8,128)(2,1)S(1)}, bf16[4,64,128]{2,1,0:T(8,128)(2,1)S(1)}, bf16[4,64,128]{2,1,0:T(8,128)(2,1...) custom-call(f32[64,3072]{1,0:T(8,128)S(1)} %get-tuple-element.137.pa, ...), custom_call_target="tpu_custom_call" | custom-call | tf_op jit(solution)/shard_map/down_sweep/pallas_call | solution.py:667
  48.6 2.0 %collective-permute-start.10 = (bf16[4,64,128]{2,1,0:T(8,128)(2,1)S(1)}, bf16[4,64,128]{2,1,0:T(8,128)(2,1)S(1)}, u32[]{:S(2)}, u32[]{:S(2)}) collective-permute-start(bf16[4,64,128]{2,1,0:T(8,128)(2,1)S(1)} %get-tuple-element.172), channel_id=1, source_target_pairs={{0,4},{4,8},{8,12},{12,16},{16,20},{20,24},{24,28},{28,32},{32,36}... | collective-permute-start | bytes 196616 | tf_op jit(solution)/shard_map/ppermute | solution.py:698
  51.9 2.4 %collective-permute-done.11.rest_1_.h1 = bf16[4,64,128]{2,1,0:T(8,128)(2,1)S(1)} collective-permute-done((bf16[4,64,128]{2,1,0:T(8,128)(2,1)S(1)}, bf16[4,64,128]{2,1,0:T(8,128)(2,1)S(1)}, u32[]{:S(2)}, u32[]{:S(2)}) %collective-permute-start.11) | collective-permute-done | bytes 65568 | tf_op jit(solution)/shard_map/ppermute | solution.py:698
  54.3 2.0 %collective-permute-start.12 = (bf16[3,64,128]{2,1,0:T(8,128)(2,1)S(1)}, bf16[3,64,128]{2,1,0:T(8,128)(2,1)S(1)}, u32[]{:S(2)}, u32[]{:S(2)}) collective-permute-start(bf16[3,64,128]{2,1,0:T(8,128)(2,1)S(1)} %pad_maximum_fusion.9), channel_id=1, source_target_pairs={{0,3},{1,0},{2,1},{3,2},{4,7},{5,4},{6,5},{7,6},{8,11},{9,8},{10,9... | collective-permute-start | bytes 147464 | tf_op jit(solution)/shard_map/ppermute | solution.py:693
  58.9 2.0 %collective-permute-done.13.h4 = bf16[3,64,128]{2,1,0:T(8,128)(2,1)S(1)} collective-permute-done((bf16[3,64,128]{2,1,0:T(8,128)(2,1)S(1)}, bf16[3,64,128]{2,1,0:T(8,128)(2,1)S(1)}, u32[]{:S(2)}, u32[]{:S(2)}) %collective-permute-start.13) | collective-permute-done | bytes 49184 | tf_op jit(solution)/shard_map/ppermute | solution.py:693
  61.4 7.0 %up_backward.1 = (bf16[8,64,128]{2,1,0:T(8,128)(2,1)S(1)}, bf16[4,64,128]{2,1,0:T(8,128)(2,1)S(1)}, bf16[4,64,128]{2,1,0:T(8,128)(2,1)S(1)}, bf16[64,6144]{1,0:T...) custom-call(s32[4,48,128]{2,1,0:T(8,128)S(1)} %get-tuple-element.141.index_ref, ...), custom_call_target="tpu_custom_call" | custom-call | tf_op jit(solution)/shard_map/up_backward/pallas_call | solution.py:667
  68.4 3.9 %collective-permute-start.15 = (bf16[8,64,128]{2,1,0:T(8,128)(2,1)S(1)}, bf16[8,64,128]{2,1,0:T(8,128)(2,1)S(1)}, u32[]{:S(2)}, u32[]{:S(2)}) collective-permute-start(bf16[8,64,128]{2,1,0:T(8,128)(2,1)S(1)} %get-tuple-element.204), channel_id=1, source_target_pairs={{0,4},{4,0},{8,12},{12,8},{16,20},{20,16},{24,28},{28,24},{32,36},... | collective-permute-start | bytes 393224 | tf_op jit(solution)/shard_map/ppermute | solution.py:682
  73.3 5.3 %collective-permute-start.18 = (bf16[4,64,128]{2,1,0:T(8,128)(2,1)S(1)}, bf16[4,64,128]{2,1,0:T(8,128)(2,1)S(1)}, u32[]{:S(2)}, u32[]{:S(2)}) collective-permute-start(bf16[4,64,128]{2,1,0:T(8,128)(2,1)S(1)} %get-tuple-element.228), channel_id=1, source_target_pairs={{0,24},{4,100},{8,0},{12,108},{16,8},{20,116},{24,16},{28,124},{32... | collective-permute-start | bytes 196616 | tf_op jit(solution)/shard_map/ppermute | solution.py:717
  80.0 4.1 %collective-permute-start.19 = (bf16[4,64,128]{2,1,0:T(8,128)(2,1)S(1)}, bf16[4,64,128]{2,1,0:T(8,128)(2,1)S(1)}, u32[]{:S(2)}, u32[]{:S(2)}) collective-permute-start(bf16[4,64,128]{2,1,0:T(8,128)(2,1)S(1)} %get-tuple-element.206), channel_id=1, source_target_pairs={{4,8},{12,16},{20,24},{28,32},{36,40},{44,48},{52,56},{60,64},{68,... | collective-permute-start | bytes 196616 | tf_op jit(solution)/shard_map/ppermute | solution.py:688
  84.1 2.0 %feat_grads.1 = (f32[64,6144]{1,0:T(8,128)}, f32[64,6144]{1,0:T(8,128)}) custom-call(bf16[64,6144]{1,0:T(8,128)(2,1)S(1)} %get-tuple-element.207.up_ref, bf16[64,6144]{1,0:T(8,128)(2,1)S(1)} %get-tuple-element.177.first_ref.down_ref, bf16[2,192,64]{2,1,0:T(8,128)(2,1)S(1)} %get-tuple-element.167.w1t_ref, ...), custom_call_target="tpu_custom_call" | custom-call | tf_op jit(solution)/shard_map/feat_grads/pallas_call | solution.py:667
  86.4 2.1 %collective-permute-start.21 = (bf16[7,64,128]{2,1,0:T(8,128)(2,1)S(1)}, bf16[7,64,128]{2,1,0:T(8,128)(2,1)S(1)}, u32[]{:S(2)}, u32[]{:S(2)}) collective-permute-start(bf16[7,64,128]{2,1,0:T(8,128)(2,1)S(1)} %get-tuple-element.236), channel_id=1, source_target_pairs={{0,2},{1,3},{2,0},{3,1},{4,6},{5,7},{6,4},{7,5},{8,10},{9,11},{10,... | collective-permute-start | bytes 344072 | tf_op jit(solution)/shard_map/ppermute | solution.py:693
  89.6 3.3 %down_targets.1.start_ref = f32[64,3072]{1,0:T(8,128)S(1)} custom-call(s32[4,48,128]{2,1,0:T(8,128)S(1)} %get-tuple-element.133.index_ref, bf16[64,6144]{1,0:T(8,128)(2,1)S(1)} %get-tuple-element.177.first_ref.down_ref, f32[64,3072]{1,0:T(8,128)S(1)} %bitcast.23, bf16[256,768]{1,0:T(8,128)(2,1)S(1)} %get-tuple-element.183.table, ...), custom_call_target="tpu_custom_call" | custom-call | tf_op jit(solution)/shard_map/down_targets/pallas_call | solution.py:667
  94.8 2.6 %collective-permute-start.25 = (bf16[4,64,128]{2,1,0:T(8,128)(2,1)S(1)}, bf16[4,64,128]{2,1,0:T(8,128)(2,1)S(1)}, u32[]{:S(2)}, u32[]{:S(2)}) collective-permute-start(bf16[4,64,128]{2,1,0:T(8,128)(2,1)S(1)} %fusion), channel_id=1, source_target_pairs={{0,96},{4,28},{8,104},{12,4},{16,112},{20,12},{24,120},{28,20},{32... | collective-permute-start | bytes 196616 | tf_op jit(solution)/shard_map/ppermute | solution.py:717
  100.4 2.1 %collective-permute-done.24 = bf16[4,64,128]{2,1,0:T(8,128)(2,1)S(1)} collective-permute-done((bf16[4,64,128]{2,1,0:T(8,128)(2,1)S(1)}, bf16[4,64,128]{2,1,0:T(8,128)(2,1)S(1)}, u32[]{:S(2)}, u32[]{:S(2)}) %collective-permute-start.24) | collective-permute-done | bytes 65568 | tf_op jit(solution)/shard_map/ppermute | solution.py:717
  102.6 2.0 %collective-permute-start.26 = (bf16[4,64,128]{2,1,0:T(8,128)(2,1)S(1)}, bf16[4,64,128]{2,1,0:T(8,128)(2,1)S(1)}, u32[]{:S(2)}, u32[]{:S(2)}) collective-permute-start(bf16[4,64,128]{2,1,0:T(8,128)(2,1)S(1)} %reduce-precision_convert_fusion.own_ref), channel_id=1, source_target_pairs={{0,4},{4,0},{8,12},{12,8},{16,20},{20,16},{24,28},{28,24},{32,36},... | collective-permute-start | bytes 196616 | tf_op jit(solution)/shard_map/ppermute | solution.py:682
  (74 shorter events, 24.6 us)
Async XLA Ops:
  2.6 7.8 %collective-permute-start = (bf16[4,64,128]{2,1,0:T(8,128)(2,1)S(1)}, bf16[4,64,128]{2,1,0:T(8,128)(2,1)S(1)}, u32[]{:S(2)}, u32[]{:S(2)}) collective-permute-start(bf16[4,64,128]{2,1,0:T(8,128)(2,1)S(1)} %get-tuple-element.120), channel_id=1, source_target_pairs={{0,4},{4,0},{8,12},{12,8},{16,20},{20,16},{24,28},{28,24},{32,36},... | collective-permute-start | bytes 196616 | tf_op jit(solution)/shard_map/ppermute | solution.py:682
  4.1 6.3 %collective-permute-start.1 = (bf16[4,64,128]{2,1,0:T(8,128)(2,1)S(1)}, bf16[4,64,128]{2,1,0:T(8,128)(2,1)S(1)}, u32[]{:S(2)}, u32[]{:S(2)}) collective-permute-start(bf16[4,64,128]{2,1,0:T(8,128)(2,1)S(1)} %get-tuple-element.121), channel_id=1, source_target_pairs={{4,8},{12,16},{20,24},{28,32},{36,40},{44,48},{52,56},{60,64},{68,... | collective-permute-start | bytes 196616 | tf_op jit(solution)/shard_map/ppermute | solution.py:688
  10.5 6.8 %collective-permute-start.2 = (bf16[3,64,128]{2,1,0:T(8,128)(2,1)S(1)}, bf16[3,64,128]{2,1,0:T(8,128)(2,1)S(1)}, u32[]{:S(2)}, u32[]{:S(2)}) collective-permute-start(bf16[3,64,128]{2,1,0:T(8,128)(2,1)S(1)} %pad_maximum_fusion.3), channel_id=1, source_target_pairs={{0,1},{1,2},{2,3},{3,0},{4,5},{5,6},{6,7},{7,4},{8,9},{9,10},{10,1... | collective-permute-start | bytes 147464 | tf_op jit(solution)/shard_map/ppermute | solution.py:693
  11.9 5.4 %collective-permute-start.3 = (bf16[3,64,128]{2,1,0:T(8,128)(2,1)S(1)}, bf16[3,64,128]{2,1,0:T(8,128)(2,1)S(1)}, u32[]{:S(2)}, u32[]{:S(2)}) collective-permute-start(bf16[3,64,128]{2,1,0:T(8,128)(2,1)S(1)} %pad_maximum_fusion.4), channel_id=1, source_target_pairs={{0,2},{1,3},{2,0},{3,1},{4,6},{5,7},{6,4},{7,5},{8,10},{9,11},{10,... | collective-permute-start | bytes 147464 | tf_op jit(solution)/shard_map/ppermute | solution.py:693
  22.8 4.1 %collective-permute-start.5 = (bf16[4,64,128]{2,1,0:T(8,128)(2,1)S(1)}, bf16[4,64,128]{2,1,0:T(8,128)(2,1)S(1)}, u32[]{:S(2)}, u32[]{:S(2)}) collective-permute-start(bf16[4,64,128]{2,1,0:T(8,128)(2,1)S(1)} %get-tuple-element.155), channel_id=1, source_target_pairs={{0,4},{4,8},{8,12},{12,16},{16,20},{20,24},{24,28},{28,32},{32,36}... | collective-permute-start | bytes 196616 | tf_op jit(solution)/shard_map/ppermute | solution.py:698
  25.6 3.7 %collective-permute-start.6 = (bf16[4,64,128]{2,1,0:T(8,128)(2,1)S(1)}, bf16[4,64,128]{2,1,0:T(8,128)(2,1)S(1)}, u32[]{:S(2)}, u32[]{:S(2)}) collective-permute-start(bf16[4,64,128]{2,1,0:T(8,128)(2,1)S(1)} %get-tuple-element.156), channel_id=1, source_target_pairs={{0,124},{4,0},{8,4},{12,8},{16,12},{20,16},{24,20},{28,24},{32,28}... | collective-permute-start | bytes 196616 | tf_op jit(solution)/shard_map/ppermute | solution.py:698
  29.4 6.2 %collective-permute-start.7 = (bf16[3,64,128]{2,1,0:T(8,128)(2,1)S(1)}, bf16[3,64,128]{2,1,0:T(8,128)(2,1)S(1)}, u32[]{:S(2)}, u32[]{:S(2)}) collective-permute-start(bf16[3,64,128]{2,1,0:T(8,128)(2,1)S(1)} %pad_maximum_fusion.6), channel_id=1, source_target_pairs={{0,1},{1,2},{2,3},{3,0},{4,5},{5,6},{6,7},{7,4},{8,9},{9,10},{10,1... | collective-permute-start | bytes 147464 | tf_op jit(solution)/shard_map/ppermute | solution.py:693
  29.9 6.1 %collective-permute-start.8 = (bf16[3,64,128]{2,1,0:T(8,128)(2,1)S(1)}, bf16[3,64,128]{2,1,0:T(8,128)(2,1)S(1)}, u32[]{:S(2)}, u32[]{:S(2)}) collective-permute-start(bf16[3,64,128]{2,1,0:T(8,128)(2,1)S(1)} %pad_maximum_fusion.7), channel_id=1, source_target_pairs={{0,2},{1,3},{2,0},{3,1},{4,6},{5,7},{6,4},{7,5},{8,10},{9,11},{10,... | collective-permute-start | bytes 147464 | tf_op jit(solution)/shard_map/ppermute | solution.py:693
  48.6 3.3 %collective-permute-start.10 = (bf16[4,64,128]{2,1,0:T(8,128)(2,1)S(1)}, bf16[4,64,128]{2,1,0:T(8,128)(2,1)S(1)}, u32[]{:S(2)}, u32[]{:S(2)}) collective-permute-start(bf16[4,64,128]{2,1,0:T(8,128)(2,1)S(1)} %get-tuple-element.172), channel_id=1, source_target_pairs={{0,4},{4,8},{8,12},{12,16},{16,20},{20,24},{24,28},{28,32},{32,36}... | collective-permute-start | bytes 196616 | tf_op jit(solution)/shard_map/ppermute | solution.py:698
  50.6 3.7 %collective-permute-start.11 = (bf16[4,64,128]{2,1,0:T(8,128)(2,1)S(1)}, bf16[4,64,128]{2,1,0:T(8,128)(2,1)S(1)}, u32[]{:S(2)}, u32[]{:S(2)}) collective-permute-start(bf16[4,64,128]{2,1,0:T(8,128)(2,1)S(1)} %get-tuple-element.173), channel_id=1, source_target_pairs={{0,124},{4,0},{8,4},{12,8},{16,12},{20,16},{24,20},{28,24},{32,28}... | collective-permute-start | bytes 196616 | tf_op jit(solution)/shard_map/ppermute | solution.py:698
  54.3 4.6 %collective-permute-start.12 = (bf16[3,64,128]{2,1,0:T(8,128)(2,1)S(1)}, bf16[3,64,128]{2,1,0:T(8,128)(2,1)S(1)}, u32[]{:S(2)}, u32[]{:S(2)}) collective-permute-start(bf16[3,64,128]{2,1,0:T(8,128)(2,1)S(1)} %pad_maximum_fusion.9), channel_id=1, source_target_pairs={{0,3},{1,0},{2,1},{3,2},{4,7},{5,4},{6,5},{7,6},{8,11},{9,8},{10,9... | collective-permute-start | bytes 147464 | tf_op jit(solution)/shard_map/ppermute | solution.py:693
  56.3 4.6 %collective-permute-start.13 = (bf16[3,64,128]{2,1,0:T(8,128)(2,1)S(1)}, bf16[3,64,128]{2,1,0:T(8,128)(2,1)S(1)}, u32[]{:S(2)}, u32[]{:S(2)}) collective-permute-start(bf16[3,64,128]{2,1,0:T(8,128)(2,1)S(1)} %pad_maximum_fusion.10), channel_id=1, source_target_pairs={{0,2},{1,3},{2,0},{3,1},{4,6},{5,7},{6,4},{7,5},{8,10},{9,11},{10,... | collective-permute-start | bytes 147464 | tf_op jit(solution)/shard_map/ppermute | solution.py:693
  56.7 4.7 %collective-permute-start.14 = (bf16[3,64,128]{2,1,0:T(8,128)(2,1)S(1)}, bf16[3,64,128]{2,1,0:T(8,128)(2,1)S(1)}, u32[]{:S(2)}, u32[]{:S(2)}) collective-permute-start(bf16[3,64,128]{2,1,0:T(8,128)(2,1)S(1)} %pad_maximum_fusion.11), channel_id=1, source_target_pairs={{0,1},{1,2},{2,3},{3,0},{4,5},{5,6},{6,7},{7,4},{8,9},{9,10},{10,1... | collective-permute-start | bytes 147464 | tf_op jit(solution)/shard_map/ppermute | solution.py:693
  68.4 4.9 %collective-permute-start.15 = (bf16[8,64,128]{2,1,0:T(8,128)(2,1)S(1)}, bf16[8,64,128]{2,1,0:T(8,128)(2,1)S(1)}, u32[]{:S(2)}, u32[]{:S(2)}) collective-permute-start(bf16[8,64,128]{2,1,0:T(8,128)(2,1)S(1)} %get-tuple-element.204), channel_id=1, source_target_pairs={{0,4},{4,0},{8,12},{12,8},{16,20},{20,16},{24,28},{28,24},{32,36},... | collective-permute-start | bytes 393224 | tf_op jit(solution)/shard_map/ppermute | solution.py:682
  73.3 12.9 %collective-permute-start.18 = (bf16[4,64,128]{2,1,0:T(8,128)(2,1)S(1)}, bf16[4,64,128]{2,1,0:T(8,128)(2,1)S(1)}, u32[]{:S(2)}, u32[]{:S(2)}) collective-permute-start(bf16[4,64,128]{2,1,0:T(8,128)(2,1)S(1)} %get-tuple-element.228), channel_id=1, source_target_pairs={{0,24},{4,100},{8,0},{12,108},{16,8},{20,116},{24,16},{28,124},{32... | collective-permute-start | bytes 196616 | tf_op jit(solution)/shard_map/ppermute | solution.py:717
  78.6 7.6 %collective-permute-start.17 = (bf16[4,64,128]{2,1,0:T(8,128)(2,1)S(1)}, bf16[4,64,128]{2,1,0:T(8,128)(2,1)S(1)}, u32[]{:S(2)}, u32[]{:S(2)}) collective-permute-start(bf16[4,64,128]{2,1,0:T(8,128)(2,1)S(1)} %get-tuple-element.228), channel_id=1, source_target_pairs={{0,8},{4,36},{8,16},{12,44},{16,24},{20,52},{24,0},{28,60},{32,40}... | collective-permute-start | bytes 196616 | tf_op jit(solution)/shard_map/ppermute | solution.py:717
  78.6 7.6 %collective-permute-start.16 = (bf16[4,64,128]{2,1,0:T(8,128)(2,1)S(1)}, bf16[4,64,128]{2,1,0:T(8,128)(2,1)S(1)}, u32[]{:S(2)}, u32[]{:S(2)}) collective-permute-start(bf16[4,64,128]{2,1,0:T(8,128)(2,1)S(1)} %get-tuple-element.228), channel_id=1, source_target_pairs={{0,16},{4,68},{8,24},{12,76},{16,0},{20,84},{24,8},{28,92},{32,48}... | collective-permute-start | bytes 196616 | tf_op jit(solution)/shard_map/ppermute | solution.py:717
  80.0 6.2 %collective-permute-start.19 = (bf16[4,64,128]{2,1,0:T(8,128)(2,1)S(1)}, bf16[4,64,128]{2,1,0:T(8,128)(2,1)S(1)}, u32[]{:S(2)}, u32[]{:S(2)}) collective-permute-start(bf16[4,64,128]{2,1,0:T(8,128)(2,1)S(1)} %get-tuple-element.206), channel_id=1, source_target_pairs={{4,8},{12,16},{20,24},{28,32},{36,40},{44,48},{52,56},{60,64},{68,... | collective-permute-start | bytes 196616 | tf_op jit(solution)/shard_map/ppermute | solution.py:688
  86.3 7.6 %collective-permute-start.22 = (bf16[7,64,128]{2,1,0:T(8,128)(2,1)S(1)}, bf16[7,64,128]{2,1,0:T(8,128)(2,1)S(1)}, u32[]{:S(2)}, u32[]{:S(2)}) collective-permute-start(bf16[7,64,128]{2,1,0:T(8,128)(2,1)S(1)} %get-tuple-element.235), channel_id=1, source_target_pairs={{0,1},{1,2},{2,3},{3,0},{4,5},{5,6},{6,7},{7,4},{8,9},{9,10},{10,1... | collective-permute-start | bytes 344072 | tf_op jit(solution)/shard_map/ppermute | solution.py:693
  86.4 7.5 %collective-permute-start.21 = (bf16[7,64,128]{2,1,0:T(8,128)(2,1)S(1)}, bf16[7,64,128]{2,1,0:T(8,128)(2,1)S(1)}, u32[]{:S(2)}, u32[]{:S(2)}) collective-permute-start(bf16[7,64,128]{2,1,0:T(8,128)(2,1)S(1)} %get-tuple-element.236), channel_id=1, source_target_pairs={{0,2},{1,3},{2,0},{3,1},{4,6},{5,7},{6,4},{7,5},{8,10},{9,11},{10,... | collective-permute-start | bytes 344072 | tf_op jit(solution)/shard_map/ppermute | solution.py:693
  88.5 6.2 %collective-permute-start.20 = (bf16[7,64,128]{2,1,0:T(8,128)(2,1)S(1)}, bf16[7,64,128]{2,1,0:T(8,128)(2,1)S(1)}, u32[]{:S(2)}, u32[]{:S(2)}) collective-permute-start(bf16[7,64,128]{2,1,0:T(8,128)(2,1)S(1)} %get-tuple-element.237), channel_id=1, source_target_pairs={{0,3},{1,0},{2,1},{3,2},{4,7},{5,4},{6,5},{7,6},{8,11},{9,8},{10,9... | collective-permute-start | bytes 344072 | tf_op jit(solution)/shard_map/ppermute | solution.py:693
  94.8 5.6 %collective-permute-start.25 = (bf16[4,64,128]{2,1,0:T(8,128)(2,1)S(1)}, bf16[4,64,128]{2,1,0:T(8,128)(2,1)S(1)}, u32[]{:S(2)}, u32[]{:S(2)}) collective-permute-start(bf16[4,64,128]{2,1,0:T(8,128)(2,1)S(1)} %fusion), channel_id=1, source_target_pairs={{0,96},{4,28},{8,104},{12,4},{16,112},{20,12},{24,120},{28,20},{32... | collective-permute-start | bytes 196616 | tf_op jit(solution)/shard_map/ppermute | solution.py:717
  97.4 5.0 %collective-permute-start.24 = (bf16[4,64,128]{2,1,0:T(8,128)(2,1)S(1)}, bf16[4,64,128]{2,1,0:T(8,128)(2,1)S(1)}, u32[]{:S(2)}, u32[]{:S(2)}) collective-permute-start(bf16[4,64,128]{2,1,0:T(8,128)(2,1)S(1)} %fusion), channel_id=1, source_target_pairs={{0,32},{4,12},{8,40},{12,20},{16,48},{20,28},{24,56},{28,4},{32,64... | collective-permute-start | bytes 196616 | tf_op jit(solution)/shard_map/ppermute | solution.py:717
  97.4 5.0 %collective-permute-start.23 = (bf16[4,64,128]{2,1,0:T(8,128)(2,1)S(1)}, bf16[4,64,128]{2,1,0:T(8,128)(2,1)S(1)}, u32[]{:S(2)}, u32[]{:S(2)}) collective-permute-start(bf16[4,64,128]{2,1,0:T(8,128)(2,1)S(1)} %fusion), channel_id=1, source_target_pairs={{0,64},{4,20},{8,72},{12,28},{16,80},{20,4},{24,88},{28,12},{32,96... | collective-permute-start | bytes 196616 | tf_op jit(solution)/shard_map/ppermute | solution.py:717
  (5 other events, 26.9 us)

commit v2 on v1

--- a/solution.py
+++ b/solution.py
@@ -825,7 +825,6 @@
 
     partner = core_swap(partner)
     total = rounded(rounded(keep) + partner[4:].astype(F32))
-    cross, keep = lax.optimization_barrier((cross, total))
     cross = cross_swap(cross)
     total = sum_along(total, (2, 8))
     feat_grad_up, feat_grad_down = call(

time: 106 us -> 109 us (1.028)
  waiting for transfers between devices: 16.6 us -> 19 us
    ppermute x6, waiting for transfers between devices: 2.07 us -> 4.47 us  [chip_ring(): return lax.ppermute(block, 'band', pairs)]
    ppermute x3, starting transfers between devices: 7.44 us -> 6.34 us  [core_swap(): lax.ppermute(block, 'band', [(i, i ^ 1) for i in range(lax.axis_size('ban...]
  transfers between devices with their start and end apart: 27 -> 27, of which waited for: 14 -> 16; matrix products, arithmetic and copies ran while one was open for 0% -> 0% of each run, Pallas kernels for 14% -> 14%
where the time goes in v2:
time: 109 us
  starting transfers between devices  46.1 us (42%)
  Pallas kernels  42.4 us (39%)
  waiting for transfers between devices  19 us (17%)
    pallas_call x13, Pallas kernels, run(): pl.pallas_call(kernel, name=name, grid=(steps,) if streamed else (), in_s...  42.4 us
    ppermute x12, starting transfers between devices, along_level(): lax.ppermute(block, 'level', [(i, (i + step) % count) for i in range(coun...  15.4 us
    ppermute x6, starting transfers between devices, chip_ring(): return lax.ppermute(block, 'band', pairs)  11.6 us
    ppermute x2, starting transfers between devices, cross_swap(): lax.ppermute(block, 'band', pairs + [(b, a) for a, b in pairs] + [(0, 0),...  7.91 us
    ppermute x4, waiting for transfers between devices, along_band(): lax.ppermute(block, 'band', [(i, (i + step) % count) for i in range(count)])  7.37 us
    ppermute x3, starting transfers between devices, core_swap(): lax.ppermute(block, 'band', [(i, i ^ 1) for i in range(lax.axis_size('ban...  6.34 us
    ppermute x12, waiting for transfers between devices, along_level(): lax.ppermute(block, 'level', [(i, (i + step) % count) for i in range(coun...  5.09 us
    ppermute x4, starting transfers between devices, along_band(): lax.ppermute(block, 'band', [(i, (i + step) % count) for i in range(count)])  4.84 us
  transfers between devices with their start and end apart: 27, of which 16 were waited for; matrix products, arithmetic and copies ran while one was open for 0% of the time, Pallas kernels for 14%

profile of v2, /device:TPU:1, one launch (start us, length us, event | category | flops | bytes accessed | tf_op | source)
XLA Modules:
  0.0 108.9 jit_solution(11258032584649214819)
XLA Ops:
  0.7 2.0 %send_lower.1 = (bf16[4,64,128]{2,1,0:T(8,128)(2,1)S(1)}, bf16[4,64,128]{2,1,0:T(8,128)(2,1)S(1)}, bf16[4,64,128]{2,1,0:T(8,128)(2,1)S(1)}, s32[12,128]{1,0:T(8,...) custom-call(s32[12,128]{1,0:T(8,128)} %refs_0_.1, ...), custom_call_target="tpu_custom_call" | custom-call | tf_op jit(solution)/shard_map/send_lower/pallas_call | solution.py:667
  4.1 3.5 %collective-permute-start.1 = (bf16[4,64,128]{2,1,0:T(8,128)(2,1)S(1)}, bf16[4,64,128]{2,1,0:T(8,128)(2,1)S(1)}, u32[]{:S(2)}, u32[]{:S(2)}) collective-permute-start(bf16[4,64,128]{2,1,0:T(8,128)(2,1)S(1)} %get-tuple-element.120), channel_id=1, source_target_pairs={{4,8},{12,16},{20,24},{28,32},{36,40},{44,48},{52,56},{60,64},{68,... | collective-permute-start | bytes 196616 | tf_op jit(solution)/shard_map/ppermute | solution.py:688
  8.5 1.9 %part_down_a.1 = (f32[64,3072]{1,0:T(8,128)S(1)}, bf16[128,3072]{1,0:T(8,128)(2,1)S(1)}) custom-call(s32[4,48,128]{2,1,0:T(8,128)S(1)} %get-tuple-element.132.index_ref, bf16[64,6144]{1,0:T(8,128)(2,1)} %bitcast.25, bf16[64,3072]{1,0:T(8,128)(2,1)S(1)} %get-tuple-element.133.local_ref, bf16[2,64,192]{2,1,0:T(8,128)(2,1)S(1)} %get-tuple-element.126.w1_ref, ...), custom_call_target="tpu_custom_call" | custom-call | tf_op jit(solution)/shard_map/part_down_a/pallas_call | solution.py:667
  11.9 2.7 %collective-permute-start.3 = (bf16[3,64,128]{2,1,0:T(8,128)(2,1)S(1)}, bf16[3,64,128]{2,1,0:T(8,128)(2,1)S(1)}, u32[]{:S(2)}, u32[]{:S(2)}) collective-permute-start(bf16[3,64,128]{2,1,0:T(8,128)(2,1)S(1)} %pad_maximum_fusion.4), channel_id=1, source_target_pairs={{0,2},{1,3},{2,0},{3,1},{4,6},{5,7},{6,4},{7,5},{8,10},{9,11},{10,... | collective-permute-start | bytes 147464 | tf_op jit(solution)/shard_map/ppermute | solution.py:693
  17.6 5.2 %up_forward.1 = (f32[64,768]{1,0:T(8,128)}, bf16[64,768]{1,0:T(8,128)(2,1)S(1)}, bf16[4,64,128]{2,1,0:T(8,128)(2,1)S(1)}, bf16[4,64,128]{2,1,0:T(8,128)(2,1)S(1)...) custom-call(f32[64,6144]{1,0:T(8,128)S(1)} %get-tuple-element.143.pa, ...), custom_call_target="tpu_custom_call" | custom-call | tf_op jit(solution)/shard_map/up_forward/pallas_call | solution.py:667
  22.8 2.8 %collective-permute-start.5 = (bf16[4,64,128]{2,1,0:T(8,128)(2,1)S(1)}, bf16[4,64,128]{2,1,0:T(8,128)(2,1)S(1)}, u32[]{:S(2)}, u32[]{:S(2)}) collective-permute-start(bf16[4,64,128]{2,1,0:T(8,128)(2,1)S(1)} %get-tuple-element.154), channel_id=1, source_target_pairs={{0,4},{4,8},{8,12},{12,16},{16,20},{20,24},{24,28},{28,32},{32,36}... | collective-permute-start | bytes 196616 | tf_op jit(solution)/shard_map/ppermute | solution.py:698
  27.0 2.4 %collective-permute-done.6.rest_1_.r1 = bf16[4,64,128]{2,1,0:T(8,128)(2,1)S(1)} collective-permute-done((bf16[4,64,128]{2,1,0:T(8,128)(2,1)S(1)}, bf16[4,64,128]{2,1,0:T(8,128)(2,1)S(1)}, u32[]{:S(2)}, u32[]{:S(2)}) %collective-permute-start.6) | collective-permute-done | bytes 65568 | tf_op jit(solution)/shard_map/ppermute | solution.py:698
  29.9 3.1 %collective-permute-start.8 = (bf16[3,64,128]{2,1,0:T(8,128)(2,1)S(1)}, bf16[3,64,128]{2,1,0:T(8,128)(2,1)S(1)}, u32[]{:S(2)}, u32[]{:S(2)}) collective-permute-start(bf16[3,64,128]{2,1,0:T(8,128)(2,1)S(1)} %pad_maximum_fusion.7), channel_id=1, source_target_pairs={{0,2},{1,3},{2,0},{3,1},{4,6},{5,7},{6,4},{7,5},{8,10},{9,11},{10,... | collective-permute-start | bytes 147464 | tf_op jit(solution)/shard_map/ppermute | solution.py:693
  33.6 1.9 %part_down_b.1 = (f32[64,3072]{1,0:T(8,128)S(1)}, bf16[128,3072]{1,0:T(8,128)(2,1)S(1)}) custom-call(s32[4,48,128]{2,1,0:T(8,128)S(1)} %get-tuple-element.132.index_ref, bf16[64,6144]{1,0:T(8,128)(2,1)} %bitcast.26, bf16[64,3072]{1,0:T(8,128)(2,1)S(1)} %get-tuple-element.133.local_ref, bf16[2,64,192]{2,1,0:T(8,128)(2,1)S(1)} %get-tuple-element.126.w1_ref, ...), custom_call_target="tpu_custom_call" | custom-call | tf_op jit(solution)/shard_map/part_down_b/pallas_call | solution.py:667
  36.2 12.3 %down_sweep.1 = (f32[64,3072]{1,0:T(8,128)}, bf16[4,64,128]{2,1,0:T(8,128)(2,1)S(1)}, bf16[4,64,128]{2,1,0:T(8,128)(2,1)S(1)}, bf16[4,64,128]{2,1,0:T(8,128)(2,1...) custom-call(f32[64,3072]{1,0:T(8,128)S(1)} %get-tuple-element.136.pa, ...), custom_call_target="tpu_custom_call" | custom-call | tf_op jit(solution)/shard_map/down_sweep/pallas_call | solution.py:667
  48.6 2.0 %collective-permute-start.10 = (bf16[4,64,128]{2,1,0:T(8,128)(2,1)S(1)}, bf16[4,64,128]{2,1,0:T(8,128)(2,1)S(1)}, u32[]{:S(2)}, u32[]{:S(2)}) collective-permute-start(bf16[4,64,128]{2,1,0:T(8,128)(2,1)S(1)} %get-tuple-element.171), channel_id=1, source_target_pairs={{0,4},{4,8},{8,12},{12,16},{16,20},{20,24},{24,28},{28,32},{32,36}... | collective-permute-start | bytes 196616 | tf_op jit(solution)/shard_map/ppermute | solution.py:698
  51.9 2.4 %collective-permute-done.11.rest_1_.h1 = bf16[4,64,128]{2,1,0:T(8,128)(2,1)S(1)} collective-permute-done((bf16[4,64,128]{2,1,0:T(8,128)(2,1)S(1)}, bf16[4,64,128]{2,1,0:T(8,128)(2,1)S(1)}, u32[]{:S(2)}, u32[]{:S(2)}) %collective-permute-start.11) | collective-permute-done | bytes 65568 | tf_op jit(solution)/shard_map/ppermute | solution.py:698
  54.3 2.0 %collective-permute-start.12 = (bf16[3,64,128]{2,1,0:T(8,128)(2,1)S(1)}, bf16[3,64,128]{2,1,0:T(8,128)(2,1)S(1)}, u32[]{:S(2)}, u32[]{:S(2)}) collective-permute-start(bf16[3,64,128]{2,1,0:T(8,128)(2,1)S(1)} %pad_maximum_fusion.9), channel_id=1, source_target_pairs={{0,3},{1,0},{2,1},{3,2},{4,7},{5,4},{6,5},{7,6},{8,11},{9,8},{10,9... | collective-permute-start | bytes 147464 | tf_op jit(solution)/shard_map/ppermute | solution.py:693
  57.0 1.8 %down_rest.1.packed_down_ref = f32[4,64,128]{2,1,0:T(8,128)S(1)} custom-call(bf16[128,3072]{1,0:T(8,128)(2,1)S(1)} %get-tuple-element.174.rows_a, bf16[128,3072]{1,0:T(8,128)(2,1)S(1)} %get-tuple-element.175.rows_b, bf16[64,6144]{1,0:T(8,128)(2,1)S(1)} %get-tuple-element.176.first_ref.down_ref, bf16[64,6144]{1,0:T(8,128)(2,1)S(1)} %get-tuple-element.177.second_ref, ...), custom_call_target="tpu_custom_call" | custom-call | tf_op jit(solution)/shard_map/down_rest/pallas_call | solution.py:667
  58.9 2.0 %collective-permute-done.13.h4 = bf16[3,64,128]{2,1,0:T(8,128)(2,1)S(1)} collective-permute-done((bf16[3,64,128]{2,1,0:T(8,128)(2,1)S(1)}, bf16[3,64,128]{2,1,0:T(8,128)(2,1)S(1)}, u32[]{:S(2)}, u32[]{:S(2)}) %collective-permute-start.13) | collective-permute-done | bytes 49184 | tf_op jit(solution)/shard_map/ppermute | solution.py:693
  61.3 7.0 %up_backward.1 = (bf16[8,64,128]{2,1,0:T(8,128)(2,1)S(1)}, bf16[4,64,128]{2,1,0:T(8,128)(2,1)S(1)}, bf16[4,64,128]{2,1,0:T(8,128)(2,1)S(1)}, bf16[64,6144]{1,0:T...) custom-call(s32[4,48,128]{2,1,0:T(8,128)S(1)} %get-tuple-element.140.index_ref, ...), custom_call_target="tpu_custom_call" | custom-call | tf_op jit(solution)/shard_map/up_backward/pallas_call | solution.py:667
  68.3 4.4 %collective-permute-start.19 = (bf16[4,64,128]{2,1,0:T(8,128)(2,1)S(1)}, bf16[4,64,128]{2,1,0:T(8,128)(2,1)S(1)}, u32[]{:S(2)}, u32[]{:S(2)}) collective-permute-start(bf16[4,64,128]{2,1,0:T(8,128)(2,1)S(1)} %get-tuple-element.204), channel_id=1, source_target_pairs={{4,8},{12,16},{20,24},{28,32},{36,40},{44,48},{52,56},{60,64},{68,... | collective-permute-start | bytes 196616 | tf_op jit(solution)/shard_map/ppermute | solution.py:688
  74.2 8.6 %collective-permute-start.18 = (bf16[4,64,128]{2,1,0:T(8,128)(2,1)S(1)}, bf16[4,64,128]{2,1,0:T(8,128)(2,1)S(1)}, u32[]{:S(2)}, u32[]{:S(2)}) collective-permute-start(bf16[4,64,128]{2,1,0:T(8,128)(2,1)S(1)} %fusion), channel_id=1, source_target_pairs={{0,24},{4,100},{8,0},{12,108},{16,8},{20,116},{24,16},{28,124},{32... | collective-permute-start | bytes 196616 | tf_op jit(solution)/shard_map/ppermute | solution.py:717
  84.3 2.0 %feat_grads.1 = (f32[64,6144]{1,0:T(8,128)}, f32[64,6144]{1,0:T(8,128)}) custom-call(bf16[64,6144]{1,0:T(8,128)(2,1)S(1)} %get-tuple-element.205.up_ref, bf16[64,6144]{1,0:T(8,128)(2,1)S(1)} %get-tuple-element.176.first_ref.down_ref, bf16[2,192,64]{2,1,0:T(8,128)(2,1)S(1)} %get-tuple-element.166.w1t_ref, ...), custom_call_target="tpu_custom_call" | custom-call | tf_op jit(solution)/shard_map/feat_grads/pallas_call | solution.py:667
  88.1 2.2 %collective-permute-start.21 = (bf16[7,64,128]{2,1,0:T(8,128)(2,1)S(1)}, bf16[7,64,128]{2,1,0:T(8,128)(2,1)S(1)}, u32[]{:S(2)}, u32[]{:S(2)}) collective-permute-start(bf16[7,64,128]{2,1,0:T(8,128)(2,1)S(1)} %get-tuple-element.232), channel_id=1, source_target_pairs={{0,2},{1,3},{2,0},{3,1},{4,6},{5,7},{6,4},{7,5},{8,10},{9,11},{10,... | collective-permute-start | bytes 344072 | tf_op jit(solution)/shard_map/ppermute | solution.py:693
  91.3 3.4 %down_targets.1.start_ref = f32[64,3072]{1,0:T(8,128)S(1)} custom-call(s32[4,48,128]{2,1,0:T(8,128)S(1)} %get-tuple-element.132.index_ref, bf16[64,6144]{1,0:T(8,128)(2,1)S(1)} %get-tuple-element.176.first_ref.down_ref, f32[64,3072]{1,0:T(8,128)S(1)} %bitcast.23, bf16[256,768]{1,0:T(8,128)(2,1)S(1)} %get-tuple-element.182.table, ...), custom_call_target="tpu_custom_call" | custom-call | tf_op jit(solution)/shard_map/down_targets/pallas_call | solution.py:667
  97.9 1.7 %lower_grad.1 = f32[64,3072]{1,0:T(8,128)} custom-call(bf16[8,64,128]{2,1,0:T(8,128)(2,1)S(1)} %collective-permute-done.15.rest_0_.h0, bf16[4,64,128]{2,1,0:T(8,128)(2,1)S(1)} %collective-permute-done.19.h1, bf16[4,64,128]{2,1,0:T(8,128)(2,1)S(1)} %get-tuple-element.209.h2, bf16[7,64,128]{2,1,0:T(8,128)(2,1)S(1)} %collective-permute-done.20.h3, ...), custom_call_target="tpu_custom_call" | custom-call | tf_op jit(solution)/shard_map/lower_grad/pallas_call | solution.py:667
  100.9 1.7 %collective-permute-done.23 = bf16[4,64,128]{2,1,0:T(8,128)(2,1)S(1)} collective-permute-done((bf16[4,64,128]{2,1,0:T(8,128)(2,1)S(1)}, bf16[4,64,128]{2,1,0:T(8,128)(2,1)S(1)}, u32[]{:S(2)}, u32[]{:S(2)}) %collective-permute-start.23) | collective-permute-done | bytes 65568 | tf_op jit(solution)/shard_map/ppermute | solution.py:717
  102.6 4.6 %collective-permute-start.26 = (bf16[4,64,128]{2,1,0:T(8,128)(2,1)S(1)}, bf16[4,64,128]{2,1,0:T(8,128)(2,1)S(1)}, u32[]{:S(2)}, u32[]{:S(2)}) collective-permute-start(bf16[4,64,128]{2,1,0:T(8,128)(2,1)S(1)} %reduce-precision_convert_fusion.own_ref), channel_id=1, source_target_pairs={{0,4},{4,0},{8,12},{12,8},{16,20},{20,16},{24,28},{28,24},{32,36},... | collective-permute-start | bytes 196616 | tf_op jit(solution)/shard_map/ppermute | solution.py:682
  (74 shorter events, 24.3 us)
Async XLA Ops:
  2.6 7.8 %collective-permute-start = (bf16[4,64,128]{2,1,0:T(8,128)(2,1)S(1)}, bf16[4,64,128]{2,1,0:T(8,128)(2,1)S(1)}, u32[]{:S(2)}, u32[]{:S(2)}) collective-permute-start(bf16[4,64,128]{2,1,0:T(8,128)(2,1)S(1)} %get-tuple-element.119), channel_id=1, source_target_pairs={{0,4},{4,0},{8,12},{12,8},{16,20},{20,16},{24,28},{28,24},{32,36},... | collective-permute-start | bytes 196616 | tf_op jit(solution)/shard_map/ppermute | solution.py:682
  4.1 6.3 %collective-permute-start.1 = (bf16[4,64,128]{2,1,0:T(8,128)(2,1)S(1)}, bf16[4,64,128]{2,1,0:T(8,128)(2,1)S(1)}, u32[]{:S(2)}, u32[]{:S(2)}) collective-permute-start(bf16[4,64,128]{2,1,0:T(8,128)(2,1)S(1)} %get-tuple-element.120), channel_id=1, source_target_pairs={{4,8},{12,16},{20,24},{28,32},{36,40},{44,48},{52,56},{60,64},{68,... | collective-permute-start | bytes 196616 | tf_op jit(solution)/shard_map/ppermute | solution.py:688
  10.5 6.8 %collective-permute-start.2 = (bf16[3,64,128]{2,1,0:T(8,128)(2,1)S(1)}, bf16[3,64,128]{2,1,0:T(8,128)(2,1)S(1)}, u32[]{:S(2)}, u32[]{:S(2)}) collective-permute-start(bf16[3,64,128]{2,1,0:T(8,128)(2,1)S(1)} %pad_maximum_fusion.3), channel_id=1, source_target_pairs={{0,1},{1,2},{2,3},{3,0},{4,5},{5,6},{6,7},{7,4},{8,9},{9,10},{10,1... | collective-permute-start | bytes 147464 | tf_op jit(solution)/shard_map/ppermute | solution.py:693
  11.9 5.4 %collective-permute-start.3 = (bf16[3,64,128]{2,1,0:T(8,128)(2,1)S(1)}, bf16[3,64,128]{2,1,0:T(8,128)(2,1)S(1)}, u32[]{:S(2)}, u32[]{:S(2)}) collective-permute-start(bf16[3,64,128]{2,1,0:T(8,128)(2,1)S(1)} %pad_maximum_fusion.4), channel_id=1, source_target_pairs={{0,2},{1,3},{2,0},{3,1},{4,6},{5,7},{6,4},{7,5},{8,10},{9,11},{10,... | collective-permute-start | bytes 147464 | tf_op jit(solution)/shard_map/ppermute | solution.py:693
  22.8 4.1 %collective-permute-start.5 = (bf16[4,64,128]{2,1,0:T(8,128)(2,1)S(1)}, bf16[4,64,128]{2,1,0:T(8,128)(2,1)S(1)}, u32[]{:S(2)}, u32[]{:S(2)}) collective-permute-start(bf16[4,64,128]{2,1,0:T(8,128)(2,1)S(1)} %get-tuple-element.154), channel_id=1, source_target_pairs={{0,4},{4,8},{8,12},{12,16},{16,20},{20,24},{24,28},{28,32},{32,36}... | collective-permute-start | bytes 196616 | tf_op jit(solution)/shard_map/ppermute | solution.py:698
  25.7 3.7 %collective-permute-start.6 = (bf16[4,64,128]{2,1,0:T(8,128)(2,1)S(1)}, bf16[4,64,128]{2,1,0:T(8,128)(2,1)S(1)}, u32[]{:S(2)}, u32[]{:S(2)}) collective-permute-start(bf16[4,64,128]{2,1,0:T(8,128)(2,1)S(1)} %get-tuple-element.155), channel_id=1, source_target_pairs={{0,124},{4,0},{8,4},{12,8},{16,12},{20,16},{24,20},{28,24},{32,28}... | collective-permute-start | bytes 196616 | tf_op jit(solution)/shard_map/ppermute | solution.py:698
  29.4 6.2 %collective-permute-start.7 = (bf16[3,64,128]{2,1,0:T(8,128)(2,1)S(1)}, bf16[3,64,128]{2,1,0:T(8,128)(2,1)S(1)}, u32[]{:S(2)}, u32[]{:S(2)}) collective-permute-start(bf16[3,64,128]{2,1,0:T(8,128)(2,1)S(1)} %pad_maximum_fusion.6), channel_id=1, source_target_pairs={{0,1},{1,2},{2,3},{3,0},{4,5},{5,6},{6,7},{7,4},{8,9},{9,10},{10,1... | collective-permute-start | bytes 147464 | tf_op jit(solution)/shard_map/ppermute | solution.py:693
  29.9 6.1 %collective-permute-start.8 = (bf16[3,64,128]{2,1,0:T(8,128)(2,1)S(1)}, bf16[3,64,128]{2,1,0:T(8,128)(2,1)S(1)}, u32[]{:S(2)}, u32[]{:S(2)}) collective-permute-start(bf16[3,64,128]{2,1,0:T(8,128)(2,1)S(1)} %pad_maximum_fusion.7), channel_id=1, source_target_pairs={{0,2},{1,3},{2,0},{3,1},{4,6},{5,7},{6,4},{7,5},{8,10},{9,11},{10,... | collective-permute-start | bytes 147464 | tf_op jit(solution)/shard_map/ppermute | solution.py:693
  48.6 3.4 %collective-permute-start.10 = (bf16[4,64,128]{2,1,0:T(8,128)(2,1)S(1)}, bf16[4,64,128]{2,1,0:T(8,128)(2,1)S(1)}, u32[]{:S(2)}, u32[]{:S(2)}) collective-permute-start(bf16[4,64,128]{2,1,0:T(8,128)(2,1)S(1)} %get-tuple-element.171), channel_id=1, source_target_pairs={{0,4},{4,8},{8,12},{12,16},{16,20},{20,24},{24,28},{28,32},{32,36}... | collective-permute-start | bytes 196616 | tf_op jit(solution)/shard_map/ppermute | solution.py:698
  50.6 3.7 %collective-permute-start.11 = (bf16[4,64,128]{2,1,0:T(8,128)(2,1)S(1)}, bf16[4,64,128]{2,1,0:T(8,128)(2,1)S(1)}, u32[]{:S(2)}, u32[]{:S(2)}) collective-permute-start(bf16[4,64,128]{2,1,0:T(8,128)(2,1)S(1)} %get-tuple-element.172), channel_id=1, source_target_pairs={{0,124},{4,0},{8,4},{12,8},{16,12},{20,16},{24,20},{28,24},{32,28}... | collective-permute-start | bytes 196616 | tf_op jit(solution)/shard_map/ppermute | solution.py:698
  54.3 4.6 %collective-permute-start.12 = (bf16[3,64,128]{2,1,0:T(8,128)(2,1)S(1)}, bf16[3,64,128]{2,1,0:T(8,128)(2,1)S(1)}, u32[]{:S(2)}, u32[]{:S(2)}) collective-permute-start(bf16[3,64,128]{2,1,0:T(8,128)(2,1)S(1)} %pad_maximum_fusion.9), channel_id=1, source_target_pairs={{0,3},{1,0},{2,1},{3,2},{4,7},{5,4},{6,5},{7,6},{8,11},{9,8},{10,9... | collective-permute-start | bytes 147464 | tf_op jit(solution)/shard_map/ppermute | solution.py:693
  56.3 4.6 %collective-permute-start.13 = (bf16[3,64,128]{2,1,0:T(8,128)(2,1)S(1)}, bf16[3,64,128]{2,1,0:T(8,128)(2,1)S(1)}, u32[]{:S(2)}, u32[]{:S(2)}) collective-permute-start(bf16[3,64,128]{2,1,0:T(8,128)(2,1)S(1)} %pad_maximum_fusion.10), channel_id=1, source_target_pairs={{0,2},{1,3},{2,0},{3,1},{4,6},{5,7},{6,4},{7,5},{8,10},{9,11},{10,... | collective-permute-start | bytes 147464 | tf_op jit(solution)/shard_map/ppermute | solution.py:693
  56.7 4.7 %collective-permute-start.14 = (bf16[3,64,128]{2,1,0:T(8,128)(2,1)S(1)}, bf16[3,64,128]{2,1,0:T(8,128)(2,1)S(1)}, u32[]{:S(2)}, u32[]{:S(2)}) collective-permute-start(bf16[3,64,128]{2,1,0:T(8,128)(2,1)S(1)} %pad_maximum_fusion.11), channel_id=1, source_target_pairs={{0,1},{1,2},{2,3},{3,0},{4,5},{5,6},{6,7},{7,4},{8,9},{9,10},{10,1... | collective-permute-start | bytes 147464 | tf_op jit(solution)/shard_map/ppermute | solution.py:693
  68.3 19.6 %collective-permute-start.19 = (bf16[4,64,128]{2,1,0:T(8,128)(2,1)S(1)}, bf16[4,64,128]{2,1,0:T(8,128)(2,1)S(1)}, u32[]{:S(2)}, u32[]{:S(2)}) collective-permute-start(bf16[4,64,128]{2,1,0:T(8,128)(2,1)S(1)} %get-tuple-element.204), channel_id=1, source_target_pairs={{4,8},{12,16},{20,24},{28,32},{36,40},{44,48},{52,56},{60,64},{68,... | collective-permute-start | bytes 196616 | tf_op jit(solution)/shard_map/ppermute | solution.py:688
  74.2 12.1 %collective-permute-start.18 = (bf16[4,64,128]{2,1,0:T(8,128)(2,1)S(1)}, bf16[4,64,128]{2,1,0:T(8,128)(2,1)S(1)}, u32[]{:S(2)}, u32[]{:S(2)}) collective-permute-start(bf16[4,64,128]{2,1,0:T(8,128)(2,1)S(1)} %fusion), channel_id=1, source_target_pairs={{0,24},{4,100},{8,0},{12,108},{16,8},{20,116},{24,16},{28,124},{32... | collective-permute-start | bytes 196616 | tf_op jit(solution)/shard_map/ppermute | solution.py:717
  82.8 5.0 %collective-permute-start.17 = (bf16[4,64,128]{2,1,0:T(8,128)(2,1)S(1)}, bf16[4,64,128]{2,1,0:T(8,128)(2,1)S(1)}, u32[]{:S(2)}, u32[]{:S(2)}) collective-permute-start(bf16[4,64,128]{2,1,0:T(8,128)(2,1)S(1)} %fusion), channel_id=1, source_target_pairs={{0,8},{4,36},{8,16},{12,44},{16,24},{20,52},{24,0},{28,60},{32,40}... | collective-permute-start | bytes 196616 | tf_op jit(solution)/shard_map/ppermute | solution.py:717
  82.8 5.0 %collective-permute-start.16 = (bf16[4,64,128]{2,1,0:T(8,128)(2,1)S(1)}, bf16[4,64,128]{2,1,0:T(8,128)(2,1)S(1)}, u32[]{:S(2)}, u32[]{:S(2)}) collective-permute-start(bf16[4,64,128]{2,1,0:T(8,128)(2,1)S(1)} %fusion), channel_id=1, source_target_pairs={{0,16},{4,68},{8,24},{12,76},{16,0},{20,84},{24,8},{28,92},{32,48}... | collective-permute-start | bytes 196616 | tf_op jit(solution)/shard_map/ppermute | solution.py:717
  88.0 6.7 %collective-permute-start.22 = (bf16[7,64,128]{2,1,0:T(8,128)(2,1)S(1)}, bf16[7,64,128]{2,1,0:T(8,128)(2,1)S(1)}, u32[]{:S(2)}, u32[]{:S(2)}) collective-permute-start(bf16[7,64,128]{2,1,0:T(8,128)(2,1)S(1)} %get-tuple-element.231), channel_id=1, source_target_pairs={{0,1},{1,2},{2,3},{3,0},{4,5},{5,6},{6,7},{7,4},{8,9},{9,10},{10,1... | collective-permute-start | bytes 344072 | tf_op jit(solution)/shard_map/ppermute | solution.py:693
  88.1 7.6 %collective-permute-start.21 = (bf16[7,64,128]{2,1,0:T(8,128)(2,1)S(1)}, bf16[7,64,128]{2,1,0:T(8,128)(2,1)S(1)}, u32[]{:S(2)}, u32[]{:S(2)}) collective-permute-start(bf16[7,64,128]{2,1,0:T(8,128)(2,1)S(1)} %get-tuple-element.232), channel_id=1, source_target_pairs={{0,2},{1,3},{2,0},{3,1},{4,6},{5,7},{6,4},{7,5},{8,10},{9,11},{10,... | collective-permute-start | bytes 344072 | tf_op jit(solution)/shard_map/ppermute | solution.py:693
  90.3 6.0 %collective-permute-start.20 = (bf16[7,64,128]{2,1,0:T(8,128)(2,1)S(1)}, bf16[7,64,128]{2,1,0:T(8,128)(2,1)S(1)}, u32[]{:S(2)}, u32[]{:S(2)}) collective-permute-start(bf16[7,64,128]{2,1,0:T(8,128)(2,1)S(1)} %get-tuple-element.233), channel_id=1, source_target_pairs={{0,3},{1,0},{2,1},{3,2},{4,7},{5,4},{6,5},{7,6},{8,11},{9,8},{10,9... | collective-permute-start | bytes 344072 | tf_op jit(solution)/shard_map/ppermute | solution.py:693
  96.4 3.2 %collective-permute-start.25 = (bf16[4,64,128]{2,1,0:T(8,128)(2,1)S(1)}, bf16[4,64,128]{2,1,0:T(8,128)(2,1)S(1)}, u32[]{:S(2)}, u32[]{:S(2)}) collective-permute-start(bf16[4,64,128]{2,1,0:T(8,128)(2,1)S(1)} %fusion.1), channel_id=1, source_target_pairs={{0,96},{4,28},{8,104},{12,4},{16,112},{20,12},{24,120},{28,20},{32... | collective-permute-start | bytes 196616 | tf_op jit(solution)/shard_map/ppermute | solution.py:717
  96.5 4.4 %collective-permute-start.24 = (bf16[4,64,128]{2,1,0:T(8,128)(2,1)S(1)}, bf16[4,64,128]{2,1,0:T(8,128)(2,1)S(1)}, u32[]{:S(2)}, u32[]{:S(2)}) collective-permute-start(bf16[4,64,128]{2,1,0:T(8,128)(2,1)S(1)} %fusion.1), channel_id=1, source_target_pairs={{0,32},{4,12},{8,40},{12,20},{16,48},{20,28},{24,56},{28,4},{32,64... | collective-permute-start | bytes 196616 | tf_op jit(solution)/shard_map/ppermute | solution.py:717
  97.9 4.6 %collective-permute-start.23 = (bf16[4,64,128]{2,1,0:T(8,128)(2,1)S(1)}, bf16[4,64,128]{2,1,0:T(8,128)(2,1)S(1)}, u32[]{:S(2)}, u32[]{:S(2)}) collective-permute-start(bf16[4,64,128]{2,1,0:T(8,128)(2,1)S(1)} %fusion.1), channel_id=1, source_target_pairs={{0,64},{4,20},{8,72},{12,28},{16,80},{20,4},{24,88},{28,12},{32,96... | collective-permute-start | bytes 196616 | tf_op jit(solution)/shard_map/ppermute | solution.py:717
  102.6 5.5 %collective-permute-start.26 = (bf16[4,64,128]{2,1,0:T(8,128)(2,1)S(1)}, bf16[4,64,128]{2,1,0:T(8,128)(2,1)S(1)}, u32[]{:S(2)}, u32[]{:S(2)}) collective-permute-start(bf16[4,64,128]{2,1,0:T(8,128)(2,1)S(1)} %reduce-precision_convert_fusion.own_ref), channel_id=1, source_target_pairs={{0,4},{4,0},{8,12},{12,8},{16,20},{20,16},{24,28},{28,24},{32,36},... | collective-permute-start | bytes 196616 | tf_op jit(solution)/shard_map/ppermute | solution.py:682
  (5 other events, 25.4 us)
